TPU v7x, 256 devices: a whole 4x4x8 slice. The times are simulated.
256 devices in a mesh: dp: 16 (over x, y), vocab: 16 (over z, core).
Axes of the slice: x: 4, y: 4, z: 8, core: 2. Of those that a mesh axis runs over, the one named last changes fastest.
Arguments:
- hidden: bfloat16 [2048, 2048], P('dp'), may hold values from -8 to 8
- head_weight: bfloat16 [131072, 2048], P(('dp', 'vocab')), may hold values from -0.397747564 to 0.397747564
- sampled_ids: int32 [2048], replicated, may hold values from 0 to 131071
- advantage: float32 [2048], replicated, may hold values from -4 to 4
Outputs:
- log_prob: float32 [2048], P('dp')
- entropy: float32 [2048], P('dp')
- grad_hidden: float32 [2048, 2048], P('dp', 'vocab')
- grad_weight: float32 [131072, 2048], P(('dp', 'vocab'))
All inputs are finite; a program needn't handle non-finite values.
Results may differ from a plain program's by a relative error of at most 0.0028.
Values may be sent and summed in bfloat16 or wider, within the bound.
A program may use at most 128 MiB of HBM per device.

v0:
```python
import jax
import jax.numpy as jnp
from jax import lax
from jax.sharding import PartitionSpec as P

entropy_coef = 0.25


def shards(hidden, head_weight, sampled_ids, advantage):
    row_count = head_weight.shape[0]
    tok_rows = hidden.shape[0]
    first_row = (
        lax.axis_index("dp") * lax.axis_size("vocab") + lax.axis_index("vocab")
    ) * row_count
    gathered = lax.all_gather(hidden, "dp", axis=0, tiled=True)
    logits = lax.dot_general(
        gathered, head_weight, (((1,), (1,)), ((), ())), preferred_element_type=jnp.float32
    )
    columns = first_row + jnp.arange(row_count, dtype=jnp.int32)
    picked = sampled_ids[:, None] == columns[None, :]
    local_max = jnp.max(logits, axis=1)
    row_max = lax.pmax(local_max, ("dp", "vocab"))
    expon = jnp.exp(logits - row_max[:, None])
    local_total = jnp.sum(expon, axis=1)
    local_weighted = jnp.sum(expon * logits, axis=1)
    local_target = jnp.sum(jnp.where(picked, logits, jnp.zeros_like(logits)), axis=1)
    total, weighted, target = lax.psum((local_total, local_weighted, local_target), ("dp", "vocab"))
    log_total = row_max + jnp.log(total)
    mean_logit = weighted / total
    prob = jnp.exp(logits - log_total[:, None])
    grad_logits = advantage[:, None] * (picked.astype(jnp.float32) - prob) - entropy_coef * prob * (
        logits - mean_logit[:, None]
    )
    grad_low = grad_logits.astype(jnp.bfloat16)
    partial_hidden = jnp.dot(grad_low, head_weight, preferred_element_type=jnp.float32)
    grad_weight = lax.dot_general(
        grad_low, gathered, (((0,), (0,)), ((), ())), preferred_element_type=jnp.float32
    )
    feature_part = lax.psum_scatter(partial_hidden, "vocab", scatter_dimension=1, tiled=True)
    grad_hidden = lax.psum_scatter(feature_part, "dp", scatter_dimension=0, tiled=True)
    own_start = lax.axis_index("dp") * tok_rows
    log_prob = lax.dynamic_slice_in_dim(target - log_total, own_start, tok_rows)
    entropy = lax.dynamic_slice_in_dim(log_total - mean_logit, own_start, tok_rows)
    return (log_prob, entropy, grad_hidden, grad_weight)


def solution(mesh):
    placed = (P("dp", None), P(("dp", "vocab"), None), P(), P())
    return jax.shard_map(
        shards,
        mesh=mesh,
        in_specs=placed,
        out_specs=(P("dp"), P("dp"), P("dp", "vocab"), P(("dp", "vocab"), None)),
        check_vma=False,
    )
```

profile of v0, /device:TPU:1, one launch (start us, length us, event | category | flops | bytes accessed | tf_op | source)
XLA Modules:
  0.0 447.5 jit_solution(15830920276460923794)
XLA Ops:
  7.2 0.0 copy-start
  7.2 0.0 all-gather.2.cloned.1.call-start
  7.2 0.7 all-gather.2.cloned.1.call-update
  7.9 0.0 reduce-scatter.3.cloned.1.call-start
  8.0 0.0 copy-start.1
  8.0 82.1 %all-gather.2.cloned.1.call-done = bf16[2048,2048]{1,0:T(8,128)(2,1)} async-done(((bf16[128,2048]{1,0:T(8,128)(2,1)}), bf16[2048,2048]{1,0:T(8,128)(2,1)}) %all-gather.2.cloned.1.call-update) | async-done | bytes 8388624 | tf_op jit(solution)/shard_map/all_gather | solution.py:15
  90.0 0.0 copy-done
  90.0 9.4 %fusion.11 = (f32[2048]{0:T(1024)S(1)}, f32[2048,512]{0,1:T(8,128)}) fusion(bf16[2048,2048]{1,0:T(8,128)(2,1)} %all-gather.2.cloned.1.call-done, bf16[512,2048]{1,0:T(8,128)(2,1)S(1)} %copy-done), kind=kOutput, calls=%fused_computation.17 | convolution fusion | flops 4296013824 | bytes 14688256 | tf_op jit(solution)/shard_map/dot_general | solution.py:16
  99.5 0.0 copy-start.2
  99.5 75.9 %pmax.7 = f32[2048]{0:T(1024)S(1)} all-reduce(f32[2048]{0:T(1024)S(1)} %get-tuple-element.14), channel_id=1, replica_groups=mesh['dp'=16,'vocab'=16] {'dp','vocab'}, use_global_device_ids=true, to_apply=%region_3.0 | all-reduce | flops 2048 | bytes 16384 | tf_op jit(solution)/shard_map/pmax | solution.py:22
  175.3 0.0 copy-done.1
  175.3 3.1 multiply_reduce_fusion
  178.4 74.6 %all-reduce = (f32[2048]{0:T(1024)S(1)}, f32[2048]{0:T(1024)S(1)}, f32[2048]{0:T(1024)S(1)}) all-reduce(f32[2048]{0:T(1024)S(1)} %get-tuple-element.6, f32[2048]{0:T(1024)S(1)} %get-tuple-element.5, f32[2048]{0:T(1024)S(1)} %get-tuple-element.4), channel_id=1, replica_groups=mesh['dp'=16,'vocab'=16] {'dp','vocab'}, use_global_device_ids=true, to_apply=%region_1.0 | all-reduce | flops 6144 | bytes 49152 | tf_op jit(solution)/shard_map/psum | solution.py:27
  253.0 0.0 copy-done.2
  253.0 11.9 %fusion.8 = f32[2048,2048]{1,0:T(8,128)} fusion(bf16[512,2048]{1,0:T(8,128)(2,1)S(1)} %copy-done, f32[2048,512]{0,1:T(8,128)} %get-tuple-element.15, f32[2048]{0:T(1024)S(1)} %get-tuple-element.12, f32[2048]{0:T(1024)S(1)} %get-tuple-element.13, f32[2048]{0:T(1024)S(1)} %copy-done.2, s32[2048]{0:T(1024)S(1)} %copy-done.1, s32[512]{0:T(512)S(1)} %iota_add_fusion), kind=kOutput, calls=%fused_computation.15 | convolution fusion | flops 4305453056 | bytes 23103488 | tf_op jit(solution)/shard_map/dot_general | solution.py:35
  264.9 0.0 reduce-scatter.3.cloned.1.call-update
  264.9 0.2 reduce-scatter.5.cloned.1.call-start
  265.2 95.7 %reduce-scatter.3.cloned.1.call-done = f32[2048,128]{1,0:T(8,128)} async-done(((f32[2048,2048]{1,0:T(8,128)}), f32[2048,128]{1,0:T(8,128)}) %reduce-scatter.3.cloned.1.call-update) | async-done | bytes 1048592 | tf_op jit(solution)/shard_map/reduce_scatter | solution.py:39
  360.9 0.0 reduce-scatter.5.cloned.1.call-update
  360.9 0.6 dynamic-slice_subtract_fusion
  361.5 11.8 %fusion.6 = f32[512,2048]{1,0:T(8,128)} fusion(bf16[2048,2048]{1,0:T(8,128)(2,1)} %all-gather.2.cloned.1.call-done, f32[2048,512]{0,1:T(8,128)} %get-tuple-element.15, f32[2048]{0:T(1024)S(1)} %get-tuple-element.12, f32[2048]{0:T(1024)S(1)} %get-tuple-element.13, f32[2048]{0:T(1024)S(1)} %copy-done.2, s32[2048]{0:T(1024)S(1)} %copy-done.1, ...), kind=kOutput, calls=%fused_computation.14 | convolution fusion | flops 4305453056 | bytes 16812032 | tf_op jit(solution)/shard_map/dot_general | solution.py:36
  373.3 67.7 %reduce-scatter.5.cloned.1.call-done = f32[128,128]{1,0:T(8,128)} async-done(((f32[2048,128]{1,0:T(8,128)}), f32[128,128]{1,0:T(8,128)}) %reduce-scatter.5.cloned.1.call-update) | async-done | bytes 65552 | tf_op jit(solution)/shard_map/reduce_scatter | solution.py:40
  (2 shorter events, 0.0 us)
Async XLA Ops:
  7.2 82.9 %copy-start = (bf16[512,2048]{1,0:T(8,128)(2,1)S(1)}, bf16[512,2048]{1,0:T(8,128)(2,1)}, u32[]{:S(2)}) copy-start(bf16[512,2048]{1,0:T(8,128)(2,1)} %param.5) | copy-start | bytes 6291460
  7.2 82.9 %all-gather.2.cloned.1.call-start = ((), (), s32[]{:S(2)}) async-start(), calls=%async_computation.2 | async-start | bytes 8912896 | tf_op jit(solution)/shard_map/all_gather | solution.py:15
  7.9 353.0 %reduce-scatter.3.cloned.1.call-start = ((), (), s32[]{:S(2)}) async-start(), calls=%async_computation.3 | async-start | bytes 17825792 | tf_op jit(solution)/shard_map/reduce_scatter | solution.py:39
  8.0 167.4 %copy-start.1 = (s32[2048]{0:T(1024)S(1)}, s32[2048]{0:T(1024)}, u32[]{:S(2)}) copy-start(s32[2048]{0:T(1024)} %param.6) | copy-start | bytes 24580
  99.5 153.5 %copy-start.2 = (f32[2048]{0:T(1024)S(1)}, f32[2048]{0:T(1024)}, u32[]{:S(2)}) copy-start(f32[2048]{0:T(1024)} %param.7) | copy-start | bytes 24580
  264.9 176.0 %reduce-scatter.5.cloned.1.call-start = ((), (), s32[]{:S(2)}) async-start(), calls=%async_computation.4 | async-start | bytes 1114112 | tf_op jit(solution)/shard_map/reduce_scatter | solution.py:40
Sparse Core Ops, SparseCore 0:
  10.4 79.5 all-gather.1
  265.1 95.7 reduce-scatter.2
  364.9 75.9 reduce-scatter.4
where the time goes:
time: 448 us; the launch traced here: 447 us
  waiting for transfers between devices  246 us (55%)
  blocking collectives  150 us (33%)
  matrix products  33.1 us (7%)
  between operations  13.8 us (3%)
    reduce_scatter x1, waiting for transfers between devices, shards(): lax.psum_scatter(partial_hidden, 'vocab', scatter_dimension=1, tiled=True)  95.7 us
    all_gather x1, waiting for transfers between devices, shards(): gathered = lax.all_gather(hidden, 'dp', axis=0, tiled=True)  82.1 us
    pmax x1, blocking collectives, shards(): row_max = lax.pmax(local_max, ('dp', 'vocab'))  75.9 us
    psum x1, blocking collectives, shards(): lax.psum((local_total, local_weighted, local_target), ('dp', 'vocab'))  74.6 us
    reduce_scatter x1, waiting for transfers between devices, shards(): lax.psum_scatter(feature_part, 'dp', scatter_dimension=0, tiled=True)  67.7 us
    dot_general x1, matrix products, shards(): jnp.dot(grad_low, head_weight, preferred_element_type=jnp.float32)  11.9 us
    dot_general x1, matrix products, shards(): lax.dot_general(grad_low, gathered, (((0,), (0,)), ((), ())), preferred_e...  11.8 us
    dot_general x1, matrix products, shards(): lax.dot_general(gathered, head_weight, (((1,), (1,)), ((), ())), preferre...  9.42 us
  transfers between devices with their start and end apart: 3, of which 3 were waited for; matrix products, arithmetic and copies ran while one was open for 3% of the time, Pallas kernels for 0%

commit v1 on v0

v1 whole, which is shorter than its diff:
```python
import jax
import jax.numpy as jnp
from jax import lax
from jax.experimental import pallas as pl
from jax.experimental.pallas import tpu as pltpu
from jax.sharding import PartitionSpec as P

ENTROPY_COEF = 0.25
MESH = pl.DeviceIdType.MESH
F32, BF16 = jnp.float32, jnp.bfloat16

D = 2048
V = 1024
ROWS = 512
SHARD = 128
RING = 4
NZ = 8
H = 2
R = 16
BLK = 2 * RING * R
HALF = RING * R
NB = RING * H
VC = 512
NC = 512
NSEM = 128


def kernel(hid, w, ids, adv, gw_out, gh_out, lp_out, en_out,
           hall, wall, logits, grad, grad_t, pm, x1, y1, r1, x2, y2, zs, zr, st, sx, sy, sz, fin,
           ids_in, adv_in, rolled, ids_row, adv_row, stat_swap, gw_send, gw_recv, send_sem, recv_sem, z_sem, local_sem):
    dp, vo = lax.axis_index("dp"), lax.axis_index("vocab")
    x, y = lax.div(dp, RING), lax.rem(dp, RING)
    z, core = lax.div(vo, 2), lax.rem(vo, 2)
    pa, pb = x + core * (y - x), y + core * (x - y)
    a_p, a_2, a_m = (lax.rem(pa + k, RING) for k in (1, 2, 3))
    b_p, b_2, b_m = (lax.rem(pb + k, RING) for k in (1, 2, 3))

    def place(a, b):
        first, second = a * RING + b, b * RING + a
        return first + core * (second - first)

    def dev(a, b):
        return {"dp": place(a, b), "vocab": vo}

    def zdev(k):
        return {"dp": dp, "vocab": lax.rem(z + k, NZ) * 2 + core}

    sibling = {"dp": dp, "vocab": vo + 1 - 2 * core}

    copies = []

    def remote(src, dst, device, arrival=None):
        i = len(copies)
        copies.append(pltpu.make_async_remote_copy(
            src_ref=src, dst_ref=dst, send_sem=send_sem.at[i], recv_sem=recv_sem.at[i] if arrival is None else arrival,
            device_id=device, device_id_type=MESH))
        return copies[-1]

    def start(*some):
        for copy in some:
            copy.start()

    def arrive(*some):
        for copy in some:
            copy.wait_recv()

    w_rows = pl.ds(pl.multiple_of(core * ROWS, ROWS), ROWS)
    w_in = pltpu.make_async_copy(w, wall.at[w_rows], local_sem.at[0])
    small_in = [pltpu.make_async_copy(ids, ids_in, local_sem.at[1]),
                pltpu.make_async_copy(adv, adv_in, local_sem.at[2])]
    own_in = [pltpu.make_async_copy(hid.at[core, h], hall.at[h * RING + pb, :, pa], local_sem.at[3 + h])
              for h in range(H)]
    for c in [w_in] + small_in + own_in:
        c.start()

    a_dev = [dev(lax.rem(pa + k, RING), pb) for k in (1, 2, 3)]
    b_dev = [dev(pa, lax.rem(pb + k, RING)) for k in (1, 2, 3)]
    z_dev = [zdev(k) for k in range(1, NZ)]
    ap, _, am = a_dev
    bp, _, bm = b_dev
    barrier = pltpu.get_barrier_semaphore()
    z_both = [[dict(dp=dp, vocab=lax.rem(z + k, NZ) * 2 + f) for f in range(2)] for k in range(1, NZ)]
    peers = a_dev + b_dev + [d for both in z_both for d in both] + [sibling]
    for peer in peers:
        pl.semaphore_signal(barrier, inc=1, device_id=peer, device_id_type=MESH)

    w_swap = remote(wall.at[w_rows], wall.at[w_rows], sibling)

    class Gather:
        def __init__(self, h):
            kp, km, k0 = (h * RING + b for b in (b_p, b_m, pb))
            own, there = hid.at[core, h], hall.at[k0, :, pa]
            self.near = [remote(own, there, d) for d in (ap, am)]
            self.far = [remote(hall.at[k0, 0, a_m], hall.at[k0, 0, a_m], ap),
                        remote(hall.at[k0, 1, a_p], hall.at[k0, 1, a_p], am)]
            self.spread, self.pass_on = {}, {}
            for slot, src in (("own", pa), ("m", a_m), ("p", a_p), ("2", a_2)):
                ref = hall.at[k0, :, src]
                self.spread[slot] = [remote(own if slot == "own" else ref, ref, d) for d in (bp, bm)]
                one, two = hall.at[km, 0, src], hall.at[kp, 1, src]
                self.pass_on[slot] = [remote(one, one, bp), remote(two, two, bm)]

        def ring(self):
            for near, far in zip(self.near, self.far):
                arrive(near)
                start(far)

        def spread_on(self, *slots):
            for slot in slots:
                start(*self.spread[slot])

        def ring_far(self):
            arrive(*self.far)
            start(*self.spread["2"])

        def forward(self, *slots):
            for slot in slots:
                for came, on in zip(self.spread[slot], self.pass_on[slot]):
                    arrive(came)
                    start(on)

        def last(self):
            for on in self.pass_on.values():
                arrive(*on)

    g0, g1 = Gather(0), Gather(1)

    lane = lax.broadcasted_iota(jnp.int32, (8, 128), 1)

    def lanes_of(group):
        return lax.div(lane, R) == group

    def reorder(source, out):
        both = source[...].astype(F32)
        rolled[...] = jnp.where(core == 0, both, pltpu.roll(both, 64, 1))
        for b in range(RING):
            rows = [jnp.broadcast_to(rolled[pl.ds(place(a, b), 1), :], (8, 128)) for a in range(RING)]
            for h in range(H):
                line = jnp.zeros((8, 128), F32)
                for a in range(RING):
                    for s in range(2):
                        group = s * RING + a
                        shift = (group * R - h * 2 * R - s * R) % 128
                        line = jnp.where(lanes_of(group), pltpu.roll(rows[a], shift, 1), line)
                out[h * RING + b] = line[0:1].astype(out.dtype)

    first_row = dp * (2 * ROWS * NZ) + z * (2 * ROWS)

    def stats_blocks(k_one, k_two):
        token_ids = jnp.concatenate([ids_row[k_one], ids_row[k_two]], axis=1) - first_row

        def logits_step(v, peak):
            rows = pl.ds(pl.multiple_of(v * VC, VC), VC)
            tokens = jnp.concatenate([hall[k_one].reshape(BLK, D), hall[k_two].reshape(BLK, D)], axis=0)
            part = lax.dot_general(wall[rows, :], tokens, (((1,), (1,)), ((), ())), preferred_element_type=F32)
            logits[k_one, rows, :] = part[:, :BLK]
            logits[k_two, rows, :] = part[:, BLK:]
            return jnp.maximum(peak, jnp.max(part.reshape(VC // 8, 8, 2 * BLK), axis=0))

        peak = lax.fori_loop(0, V // VC, logits_step, jnp.full((8, 2 * BLK), -3e38, F32))
        peak = jnp.max(peak, axis=0, keepdims=True)
        step_rows = 256

        def sums_step(v, sums):
            start_row = pl.multiple_of(v * step_rows, step_rows)
            rows = pl.ds(start_row, step_rows)
            part = jnp.concatenate([logits[k_one, rows, :], logits[k_two, rows, :]], axis=1)
            expon = jnp.exp(part - peak)
            row = lax.broadcasted_iota(jnp.int32, part.shape, 0)
            picked = jnp.where(row == token_ids - start_row, part, 0.0)
            return tuple(s + jnp.sum(p.reshape(step_rows // 8, 8, 2 * BLK), axis=0)
                         for s, p in zip(sums, (expon, expon * part, picked)))

        zero = jnp.zeros((8, 2 * BLK), F32)
        sums = lax.fori_loop(0, V // step_rows, sums_step, (zero, zero, zero))
        sums = tuple(jnp.sum(s, axis=0, keepdims=True) for s in sums)
        for q, row in enumerate((peak,) + sums):
            st[k_one, pl.ds(q, 1), :] = row[:, :BLK]
            st[k_two, pl.ds(q, 1), :] = row[:, BLK:]

    def stats_merge(ref, slots, sent):
        arrive(*sent)
        parts = [ref[...]] + [slots[i] for i in range(len(sent))]
        peak = parts[0][:, 0:1, :]
        for p in parts[1:]:
            peak = jnp.maximum(peak, p[:, 0:1, :])
        total, weighted, target = 0.0, 0.0, 0.0
        for p in parts:
            scale = jnp.exp(p[:, 0:1, :] - peak)
            total += scale * p[:, 1:2, :]
            weighted += scale * p[:, 2:3, :]
            target += p[:, 3:4, :]
        return peak, total, weighted, target

    class Stats:
        def __init__(self, h):
            blocks = pl.ds(h * RING, RING)
            self.steps = [(st.at[blocks], sx.at[h], fin.at[0, blocks], a_dev),
                          (fin.at[0, blocks], sy.at[h], fin.at[1, blocks], b_dev),
                          (fin.at[1, blocks], sz.at[h], fin.at[2, blocks], z_dev)]
            self.sent = [[remote(ref, slots.at[i], d) for i, d in enumerate(devices)]
                         for ref, slots, _, devices in self.steps]

        def begin(self):
            start(*self.sent[0])

        def step(self, i):
            ref, slots, out, _ = self.steps[i]
            rows = stats_merge(ref, slots, self.sent[i])
            if i == 2:
                peak, total, weighted, target = rows
                rows = (peak + jnp.log(total), weighted / total, target)
            for q, row in enumerate(rows):
                out[:, pl.ds(q, 1), :] = row
            if i < 2:
                start(*self.sent[i + 1])

    s0, s1 = Stats(0), Stats(1)

    order = (b_2, b_m, b_p, pb)

    def grad_chunk(h):
        ks = [h * RING + b for b in order]
        token_ids = jnp.concatenate([ids_row[k] for k in ks], axis=1) - first_row
        advantage = jnp.concatenate([adv_row[k] for k in ks], axis=1)
        log_total = jnp.concatenate([fin[2, k, 0:1, :] for k in ks], axis=1)
        mean = jnp.concatenate([fin[2, k, 1:2, :] for k in ks], axis=1)
        step_rows = 128

        def grad_step(v, carry):
            start_row = pl.multiple_of(v * step_rows, step_rows)
            rows = pl.ds(start_row, step_rows)
            part = jnp.concatenate([logits[k, rows, :] for k in ks], axis=1)
            prob = jnp.exp(part - log_total)
            row = lax.broadcasted_iota(jnp.int32, part.shape, 0)
            onehot = jnp.where(row == token_ids - start_row, 1.0, 0.0)
            low = (advantage * (onehot - prob) - ENTROPY_COEF * prob * (part - mean)).astype(BF16)
            for j, k in enumerate(ks):
                tile = low[:, j * BLK:(j + 1) * BLK]
                grad[k, rows, :] = tile
                grad_t[j * BLK:(j + 1) * BLK, rows] = tile.T
            return carry

        lax.fori_loop(0, V // step_rows, grad_step, 0)

    def product_chunk(h):
        def product_step(n, carry):
            cols = pl.ds(pl.multiple_of(n * NC, NC), NC)
            part = jnp.dot(grad_t[...], wall[:, cols], preferred_element_type=F32)
            two_0, two_1, m_0, m_1, p_0, p_1, own_0, own_1 = (part[i * HALF:(i + 1) * HALF] for i in range(8))
            x1[h, 0, :, cols] = two_0.astype(BF16)
            x1[h, 1, :, cols] = two_1.astype(BF16)
            pm[h, 0, :, cols] = m_0
            x1[h, 2, :, cols] = m_1.astype(BF16)
            x1[h, 3, :, cols] = p_0.astype(BF16)
            pm[h, 1, :, cols] = p_1
            pm[h, 2, :, cols] = own_0
            pm[h, 3, :, cols] = own_1
            return carry

        lax.fori_loop(0, D // NC, product_step, 0)

    def chunked(rows, body):
        def step(n, carry):
            body(pl.ds(pl.multiple_of(n * 16, 16), 16))
            return carry

        lax.fori_loop(0, rows // 16, step, 0)

    def slot(a):
        return pl.ds(pl.multiple_of(a * R, R), R)

    class Reduce:
        def __init__(self, h):
            self.h = h
            self.b = [remote(x1.at[h, i], y1.at[h, i], d) for i, d in enumerate((bm, bp, bm, bp, bm, bp))]
            self.a = [remote(x2.at[h, i], y2.at[h, i], d) for i, d in enumerate(a_dev)]
            self.z = [remote(zs.at[h, z, 1 - core], zr.at[h, core, 0], sibling, z_sem.at[h, 0, core])]
            self.z += [remote(zs.at[h, lax.rem(z + k, NZ), f], zr.at[h, core, k], z_both[k - 1][f], z_sem.at[h, k, core])
                       for k in range(1, NZ) for f in range(2)]
            places = [(1 - core, 0)] + [(c, k) for k in range(1, NZ) for c in range(2)]
            self.z_in = [pltpu.make_async_remote_copy(
                src_ref=zr.at[h, c, k], dst_ref=zr.at[h, c, k], send_sem=send_sem.at[0], recv_sem=z_sem.at[h, k, c],
                device_id=sibling, device_id_type=MESH) for c, k in places]

        def begin(self):
            start(*self.b[:4])

        def relay_b(self):
            h = self.h
            for i in range(2):
                arrive(self.b[i])

                def relay(rows):
                    x1[h, 4 + i, rows, :] = (pm[h, i, rows, :] + y1[h, i, rows, :].astype(F32)).astype(BF16)

                chunked(HALF, relay)
                start(self.b[4 + i])

        def end_b(self):
            h = self.h
            arrive(*self.b[2:])
            for s, (one, two) in enumerate(((3, 4), (2, 5))):

                def total(rows):
                    r1[h, s, rows, :] = (pm[h, 2 + s, rows, :] + y1[h, one, rows, :].astype(F32)
                                         + y1[h, two, rows, :].astype(F32))

                chunked(HALF, total)
            for i, a in enumerate((a_p, a_2, a_m)):
                for s in range(2):
                    x2[h, i, s] = r1[h, s, slot(a), :].astype(BF16)
            start(self.a[1], self.a[0], self.a[2])

        def end_a(self):
            h = self.h
            arrive(*self.a)
            for s in range(2):
                for f in range(2 * NZ):
                    cols = slice(f * 128, f * 128 + 128)
                    zs[h, f // 2, f % 2, s] = r1[h, s, slot(pa), cols] + sum(
                        y2[h, i, s, :, cols].astype(F32) for i in range(RING - 1))
            zr[h, core, 0] = zs[h, z, core]
            start(*self.z)

        def end_z(self):
            h = self.h
            arrive(*self.z_in)
            for c in range(2):
                total = zr[h, c, 0]
                for k in range(1, NZ):
                    total += zr[h, c, k]
                gh_out[c, h] = total

    d0, d1 = Reduce(0), Reduce(1)

    weight_copies = [remote(gw_send.at[n], gw_recv.at[n], sibling) for n in range(D // NC)]

    def weight_part(side, n):
        rows = pl.ds(pl.multiple_of(side * ROWS, ROWS), ROWS)
        cols = pl.ds(pl.multiple_of(n * NC, NC), NC)
        lhs = jnp.concatenate([grad[k, rows, :] for k in range(NB)], axis=1)
        rhs = hall[:, :, :, :, cols].reshape(NB * BLK, NC)
        return jnp.dot(lhs, rhs, preferred_element_type=F32), cols

    def weight_other(n):
        gw_send[n] = weight_part(1 - core, n)[0]

    def weight_own(n):
        part, cols = weight_part(core, n)
        gw_out[:, cols] = part + gw_recv[n]

    stat_copy = remote(stat_swap.at[0], stat_swap.at[1], sibling)

    def own_stats():
        for q in range(2):
            line = jnp.zeros((8, 128), F32)
            for h in range(H):
                k = h * RING + pb
                log_total, mean, target = (fin[2, k, pl.ds(i, 1), :] for i in range(3))
                row = jnp.broadcast_to(target - log_total if q == 0 else log_total - mean, (8, 128))
                for s in range(2):
                    group = (h * 2 + s) + core * 4
                    shift = lax.rem(group * R + 256 - (s * RING + pa) * R, 128)
                    line = jnp.where(lanes_of(group), pltpu.roll(row, shift, 1), line)
            stat_swap[0, q] = line
        start(stat_copy)

    def own_stats_store():
        arrive(stat_copy)
        mine = lax.div(lane, 64) == core
        for q, out in enumerate((lp_out, en_out)):
            out[...] = jnp.where(mine, stat_swap[0, q], stat_swap[1, q])[0:1]

    def staged(count, before, body):
        def step(i, carry):
            for j, action in before.items():
                pl.when(i == j)(action)
            body(i)
            return carry

        lax.fori_loop(0, count, step, 0)

    for c in small_in:
        c.wait()
    reorder(ids_in, ids_row)
    reorder(adv_in, adv_row)
    pl.semaphore_wait(barrier, len(peers))
    start(*g0.near, *g0.spread["own"], *g1.near)
    for c in [w_in] + own_in:
        c.wait()
    start(w_swap)
    g0.ring()
    g0.spread_on("m", "p")
    g0.forward("own")
    g0.ring_far()
    g1.spread_on("own")
    g1.ring()
    g0.forward("m", "p", "2")
    g1.spread_on("m", "p")
    g1.forward("own")
    arrive(w_swap)

    def unit(i):
        half = lax.rem(i, 2)
        k = lax.div(i, 2) * RING
        stats_blocks(k + lax.rem(pb + half, RING), k + lax.rem(pb + 3 - half, RING))

    def before_1():
        g1.ring_far()
        g0.last()

    def before_2():
        s0.begin()
        g1.forward("m", "p")
        s0.step(0)
        g1.forward("2")

    def before_3():
        s0.step(1)
        g1.last()

    staged(4, {1: before_1, 2: before_2, 3: before_3}, unit)
    s1.begin()
    s0.step(2)

    def chunk_step(h):
        grad_chunk(h)

        @pl.when(h == 0)
        def _():
            s1.step(1)

        @pl.when(h == 1)
        def _():
            d0.relay_b()

        product_chunk(h)

    def before_chunk_1():
        d0.begin()
        s1.step(2)

    staged(H, {0: lambda: s1.step(0), 1: before_chunk_1}, chunk_step)
    d1.begin()
    own_stats()
    d0.end_b()

    def send_weight(n, *then):
        def action():
            start(weight_copies[n])
            for step in then:
                step()

        return action

    def take_weight(n, *then):
        def action():
            arrive(weight_copies[n])
            for step in then:
                step()

        return action

    staged(4, {1: send_weight(0), 2: send_weight(1, d1.relay_b), 3: send_weight(2)}, weight_other)
    start(weight_copies[3])
    d0.end_a()
    staged(4, {0: take_weight(0), 1: take_weight(1, d1.end_b), 2: take_weight(2, d0.end_z),
               3: take_weight(3, d1.end_a)}, weight_own)
    own_stats_store()
    d1.end_z()
    for copy in copies:
        copy.wait_send()


def call(hid, w, ids, adv):
    vmem = pl.BlockSpec(memory_space=pltpu.VMEM)
    anywhere = pl.BlockSpec(memory_space=pl.ANY)
    scratch = [
        pltpu.VMEM((NB, 2, RING, R, D), BF16),
        pltpu.VMEM((V, D), BF16),
        pltpu.VMEM((NB, V, BLK), F32),
        pltpu.VMEM((NB, V, BLK), BF16),
        pltpu.VMEM((RING * BLK, V), BF16),
        pltpu.VMEM((H, 4, HALF, D), F32),
        pltpu.VMEM((H, 6, HALF, D), BF16),
        pltpu.VMEM((H, 6, HALF, D), BF16),
        pltpu.VMEM((H, 2, HALF, D), F32),
        pltpu.VMEM((H, RING - 1, 2, R, D), BF16),
        pltpu.VMEM((H, RING - 1, 2, R, D), BF16),
        pltpu.VMEM((H, NZ, 2, 2, R, 128), F32),
        pltpu.VMEM((H, 2, NZ, 2, R, 128), F32),
        pltpu.VMEM((NB, 4, BLK), F32),
        pltpu.VMEM((H, RING - 1, RING, 4, BLK), F32),
        pltpu.VMEM((H, RING - 1, RING, 4, BLK), F32),
        pltpu.VMEM((H, NZ - 1, RING, 4, BLK), F32),
        pltpu.VMEM((3, NB, 4, BLK), F32),
        pltpu.VMEM((16, 128), jnp.int32),
        pltpu.VMEM((16, 128), F32),
        pltpu.VMEM((16, 128), F32),
        pltpu.VMEM((NB, 1, BLK), jnp.int32),
        pltpu.VMEM((NB, 1, BLK), F32),
        pltpu.VMEM((2, 2, 8, 128), F32),
        pltpu.VMEM((D // NC, ROWS, NC), F32),
        pltpu.VMEM((D // NC, ROWS, NC), F32),
        pltpu.SemaphoreType.DMA((NSEM,)),
        pltpu.SemaphoreType.DMA((NSEM,)),
        pltpu.SemaphoreType.DMA((H, NZ, 2)),
        pltpu.SemaphoreType.DMA((3 + H,)),
    ]
    return pl.pallas_call(
        kernel,
        out_shape=(
            pltpu.VMEM((ROWS, D), F32),
            pltpu.VMEM((2, H, 2, R, 128), F32),
            pltpu.VMEM((1, SHARD), F32),
            pltpu.VMEM((1, SHARD), F32),
        ),
        in_specs=[anywhere] * 4,
        out_specs=(vmem, vmem, vmem, vmem),
        scratch_shapes=scratch,
        compiler_params=pltpu.CompilerParams(
            collective_id=0, has_side_effects=True, vmem_limit_bytes=50 * 2**20),
    )(hid, w, ids, adv)


def shards(hidden, head_weight, sampled_ids, advantage):
    hid = hidden.reshape(2, H, 2, R, D)
    grad_weight, grad_hidden, log_prob, entropy = call(
        hid, head_weight, sampled_ids.reshape(16, 128), advantage.reshape(16, 128))
    return (log_prob.reshape(SHARD), entropy.reshape(SHARD), grad_hidden.reshape(SHARD, 128), grad_weight)


def solution(mesh):
    placed = (P("dp", None), P(("dp", "vocab"), None), P(), P())
    return jax.shard_map(
        shards,
        mesh=mesh,
        in_specs=placed,
        out_specs=(P("dp"), P("dp"), P("dp", "vocab"), P(("dp", "vocab"), None)),
        check_vma=False,
    )
```

time: 448 us -> 95.9 us (0.21)
  waiting for transfers between devices: 246 us -> 0 us
  blocking collectives: 150 us -> 0 us
  Pallas kernels: 0 us -> 91.5 us
  matrix products: 33.1 us -> 0 us
  between operations: 13.8 us -> 0.64 us
    reduce_scatter x2 -> x0, waiting for transfers between devices: 163 us -> none  [the longest x1 95.7 us: shards(): lax.psum_scatter(partial_hidden, 'vocab', scatter_dimension=1, tiled=True)]
    pallas_call x0 -> x1, Pallas kernels: none -> 91.5 us  [call(): pl.pallas_call(kernel, out_shape=(pltpu.VMEM((ROWS, D), F32), pltpu.VMEM(...]
    all_gather x1 -> x0, waiting for transfers between devices: 82.1 us -> none  [shards(): gathered = lax.all_gather(hidden, 'dp', axis=0, tiled=True)]
    pmax x1 -> x0, blocking collectives: 75.9 us -> none  [shards(): row_max = lax.pmax(local_max, ('dp', 'vocab'))]
    psum x1 -> x0, blocking collectives: 74.6 us -> none  [shards(): lax.psum((local_total, local_weighted, local_target), ('dp', 'vocab'))]
    dot_general x3 -> x0, matrix products: 33.1 us -> none  [the longest x1 11.9 us: shards(): jnp.dot(grad_low, head_weight, preferred_element_type=jnp.float32)]
  transfers between devices with their start and end apart: 3 -> 0, of which waited for: 3 -> 0; matrix products, arithmetic and copies ran while one was open for 3% -> 0% of each run, Pallas kernels for 0% -> 0%
where the time goes in v1:
time: 95.9 us; the launch traced here: 95.8 us
  Pallas kernels  91.5 us (95%)
  local copies, waits for them, and re-layouts  3.67 us (4%)
    pallas_call x1, Pallas kernels, call(): pl.pallas_call(kernel, out_shape=(pltpu.VMEM((ROWS, D), F32), pltpu.VMEM(...  91.5 us
    unnamed x4, local copies, waits for them, and re-layouts  3.67 us

profile of v1, /device:TPU:1, one launch (start us, length us, event | category | flops | bytes accessed | tf_op | source)
XLA Modules:
  0.0 95.8 jit_solution(16981779961555287304)
XLA Ops:
  0.6 91.5 %shard_map.75 = (f32[512,2048]{1,0:T(8,128)S(1)}, f32[2,2,2,16,128]{4,3,2,1,0:T(8,128)S(1)}, f32[1,128]{1,0:T(1,128)S(1)}, f32[1,128]{1,0:T(1,128)S(1)}) custom-call(bf16[2,2,2,16,2048]{4,3,2,1,0:T(8,128)(2,1)} %bitcast.9, bf16[512,2048]{1,0:T(8,128)(2,1)} %w.1, s32[16,128]{1,0:T(8,128)} %bitcast.10, f32[16,128]{1,0:T(8,128)} %bitcast.11), custom_call_target="tpu_custom_call" | custom-call | tf_op jit(solution)/shard_map/pallas_call | solution.py:511
  92.1 0.5 copy.12
  92.6 0.5 copy.13
  93.1 0.6 copy.14
  93.8 2.0 %copy.15 = f32[512,2048]{1,0:T(8,128)} copy(f32[512,2048]{1,0:T(8,128)S(1)} %get-tuple-element.15) | data formatting | bytes 8388608

commit v2 on v1

--- a/solution.py
+++ b/solution.py
@@ -22,7 +22,8 @@
 NB = RING * H
 VC = 512
 NC = 512
-NSEM = 128
+DC = D // 2
+NSEM = 144
 
 
 def kernel(hid, w, ids, adv, gw_out, gh_out, lp_out, en_out,
@@ -195,9 +196,9 @@
     class Stats:
         def __init__(self, h):
             blocks = pl.ds(h * RING, RING)
-            self.steps = [(st.at[blocks], sx.at[h], fin.at[0, blocks], a_dev),
-                          (fin.at[0, blocks], sy.at[h], fin.at[1, blocks], b_dev),
-                          (fin.at[1, blocks], sz.at[h], fin.at[2, blocks], z_dev)]
+            self.steps = [(st.at[blocks], sz.at[h], fin.at[0, blocks], z_dev),
+                          (fin.at[0, blocks], sx.at[h], fin.at[1, blocks], a_dev),
+                          (fin.at[1, blocks], sy.at[h], fin.at[2, blocks], b_dev)]
             self.sent = [[remote(ref, slots.at[i], d) for i, d in enumerate(devices)]
                          for ref, slots, _, devices in self.steps]
 
@@ -243,22 +244,24 @@
 
         lax.fori_loop(0, V // step_rows, grad_step, 0)
 
-    def product_chunk(h):
+    def product_half(h, c):
         def product_step(n, carry):
-            cols = pl.ds(pl.multiple_of(n * NC, NC), NC)
-            part = jnp.dot(grad_t[...], wall[:, cols], preferred_element_type=F32)
+            start_col = pl.multiple_of(n * NC, NC)
+            cols = pl.ds(start_col, NC)
+            part = jnp.dot(grad_t[...], wall[:, pl.ds(pl.multiple_of(c * DC + start_col, NC), NC)],
+                           preferred_element_type=F32)
             two_0, two_1, m_0, m_1, p_0, p_1, own_0, own_1 = (part[i * HALF:(i + 1) * HALF] for i in range(8))
-            x1[h, 0, :, cols] = two_0.astype(BF16)
-            x1[h, 1, :, cols] = two_1.astype(BF16)
-            pm[h, 0, :, cols] = m_0
-            x1[h, 2, :, cols] = m_1.astype(BF16)
-            x1[h, 3, :, cols] = p_0.astype(BF16)
-            pm[h, 1, :, cols] = p_1
-            pm[h, 2, :, cols] = own_0
-            pm[h, 3, :, cols] = own_1
+            x1[h, c, 0, :, cols] = two_0.astype(BF16)
+            x1[h, c, 1, :, cols] = two_1.astype(BF16)
+            pm[h, c, 0, :, cols] = m_0
+            x1[h, c, 2, :, cols] = m_1.astype(BF16)
+            x1[h, c, 3, :, cols] = p_0.astype(BF16)
+            pm[h, c, 1, :, cols] = p_1
+            pm[h, c, 2, :, cols] = own_0
+            pm[h, c, 3, :, cols] = own_1
             return carry
 
-        lax.fori_loop(0, D // NC, product_step, 0)
+        lax.fori_loop(0, DC // NC, product_step, 0)
 
     def chunked(rows, body):
         def step(n, carry):
@@ -271,68 +274,84 @@
         return pl.ds(pl.multiple_of(a * R, R), R)
 
     class Reduce:
+        def __init__(self, h, c):
+            self.at = h, c
+            self.b = [remote(x1.at[h, c, i], y1.at[h, c, i], d) for i, d in enumerate((bm, bp, bm, bp, bm, bp))]
+            self.a = [remote(x2.at[h, c, i], y2.at[h, c, i], d) for i, d in enumerate(a_dev)]
+
+        def begin(self):
+            start(*self.b[:4])
+
+        def relay_b(self):
+            h, c = self.at
+            for i in range(2):
+                arrive(self.b[i])
+
+                def relay(rows):
+                    x1[h, c, 4 + i, rows, :] = (
+                        pm[h, c, i, rows, :] + y1[h, c, i, rows, :].astype(F32)).astype(BF16)
+
+                chunked(HALF, relay)
+                start(self.b[4 + i])
+
+        def end_b(self):
+            h, c = self.at
+            arrive(*self.b[2:])
+            for s, (one, two) in enumerate(((3, 4), (2, 5))):
+
+                def total(rows):
+                    r1[h, c, s, rows, :] = (pm[h, c, 2 + s, rows, :] + y1[h, c, one, rows, :].astype(F32)
+                                            + y1[h, c, two, rows, :].astype(F32))
+
+                chunked(HALF, total)
+            for i in (1, 0, 2):
+                for s in range(2):
+                    x2[h, c, i, s] = r1[h, c, s, slot((a_p, a_2, a_m)[i]), :].astype(BF16)
+                start(self.a[i])
+
+        def end_a(self):
+            h, c = self.at
+            arrive(*self.a)
+            for s in range(2):
+                for f in range(DC // 128):
+                    cols = slice(f * 128, f * 128 + 128)
+                    zs[h, c * (NZ // 2) + f // 2, f % 2, s] = r1[h, c, s, slot(pa), cols] + sum(
+                        y2[h, c, i, s, :, cols].astype(F32) for i in range(RING - 1))
+
+    class Reduce_z:
         def __init__(self, h):
             self.h = h
-            self.b = [remote(x1.at[h, i], y1.at[h, i], d) for i, d in enumerate((bm, bp, bm, bp, bm, bp))]
-            self.a = [remote(x2.at[h, i], y2.at[h, i], d) for i, d in enumerate(a_dev)]
-            self.z = [remote(zs.at[h, z, 1 - core], zr.at[h, core, 0], sibling, z_sem.at[h, 0, core])]
-            self.z += [remote(zs.at[h, lax.rem(z + k, NZ), f], zr.at[h, core, k], z_both[k - 1][f], z_sem.at[h, k, core])
-                       for k in range(1, NZ) for f in range(2)]
+            self.sibling = remote(zs.at[h, z, 1 - core], zr.at[h, core, 0], sibling, z_sem.at[h, 0, core])
+            self.others = [[remote(zs.at[h, lax.rem(z + k, NZ), f], zr.at[h, core, k], z_both[k - 1][f],
+                                   z_sem.at[h, k, core]) for f in range(2)] for k in range(1, NZ)]
             places = [(1 - core, 0)] + [(c, k) for k in range(1, NZ) for c in range(2)]
-            self.z_in = [pltpu.make_async_remote_copy(
+            self.arrivals = [pltpu.make_async_remote_copy(
                 src_ref=zr.at[h, c, k], dst_ref=zr.at[h, c, k], send_sem=send_sem.at[0], recv_sem=z_sem.at[h, k, c],
                 device_id=sibling, device_id_type=MESH) for c, k in places]
 
-        def begin(self):
-            start(*self.b[:4])
-
-        def relay_b(self):
+        def send(self, c):
+            @pl.when(lax.div(z, NZ // 2) == c)
+            def _():
+                zr[self.h, core, 0] = zs[self.h, z, core]
+                start(self.sibling)
+
+            for k in range(1, NZ):
+
+                @pl.when(lax.div(lax.rem(z + k, NZ), NZ // 2) == c)
+                def _():
+                    start(*self.others[k - 1])
+
+        def end(self):
             h = self.h
-            for i in range(2):
-                arrive(self.b[i])
-
-                def relay(rows):
-                    x1[h, 4 + i, rows, :] = (pm[h, i, rows, :] + y1[h, i, rows, :].astype(F32)).astype(BF16)
-
-                chunked(HALF, relay)
-                start(self.b[4 + i])
-
-        def end_b(self):
-            h = self.h
-            arrive(*self.b[2:])
-            for s, (one, two) in enumerate(((3, 4), (2, 5))):
-
-                def total(rows):
-                    r1[h, s, rows, :] = (pm[h, 2 + s, rows, :] + y1[h, one, rows, :].astype(F32)
-                                         + y1[h, two, rows, :].astype(F32))
-
-                chunked(HALF, total)
-            for i, a in enumerate((a_p, a_2, a_m)):
-                for s in range(2):
-                    x2[h, i, s] = r1[h, s, slot(a), :].astype(BF16)
-            start(self.a[1], self.a[0], self.a[2])
-
-        def end_a(self):
-            h = self.h
-            arrive(*self.a)
-            for s in range(2):
-                for f in range(2 * NZ):
-                    cols = slice(f * 128, f * 128 + 128)
-                    zs[h, f // 2, f % 2, s] = r1[h, s, slot(pa), cols] + sum(
-                        y2[h, i, s, :, cols].astype(F32) for i in range(RING - 1))
-            zr[h, core, 0] = zs[h, z, core]
-            start(*self.z)
-
-        def end_z(self):
-            h = self.h
-            arrive(*self.z_in)
+            arrive(*self.arrivals)
             for c in range(2):
                 total = zr[h, c, 0]
                 for k in range(1, NZ):
                     total += zr[h, c, k]
                 gh_out[c, h] = total
 
-    d0, d1 = Reduce(0), Reduce(1)
+    d00, d01, d10, d11 = (Reduce(h, c) for h in range(H) for c in range(2))
+    z0, z1 = Reduce_z(0), Reduce_z(1)
 
     weight_copies = [remote(gw_send.at[n], gw_recv.at[n], sibling) for n in range(D // NC)]
 
@@ -394,11 +413,10 @@
     g0.spread_on("m", "p")
     g0.forward("own")
     g0.ring_far()
+    g0.forward("m", "p", "2")
     g1.spread_on("own")
     g1.ring()
-    g0.forward("m", "p", "2")
     g1.spread_on("m", "p")
-    g1.forward("own")
     arrive(w_swap)
 
     def unit(i):
@@ -407,11 +425,12 @@
         stats_blocks(k + lax.rem(pb + half, RING), k + lax.rem(pb + 3 - half, RING))
 
     def before_1():
-        g1.ring_far()
+        g1.forward("own")
         g0.last()
 
     def before_2():
         s0.begin()
+        g1.ring_far()
         g1.forward("m", "p")
         s0.step(0)
         g1.forward("2")
@@ -424,29 +443,32 @@
     s1.begin()
     s0.step(2)
 
-    def chunk_step(h):
-        grad_chunk(h)
-
-        @pl.when(h == 0)
+    def half_step(i):
+        h, c = lax.div(i, 2), lax.rem(i, 2)
+
+        @pl.when(c == 0)
         def _():
-            s1.step(1)
-
-        @pl.when(h == 1)
-        def _():
-            d0.relay_b()
-
-        product_chunk(h)
-
-    def before_chunk_1():
-        d0.begin()
+            grad_chunk(h)
+
+        pl.when(i == 2)(d01.relay_b)
+        product_half(h, c)
+
+    def before_half_1():
+        d00.begin()
+        s1.step(0)
+
+    def before_half_2():
+        d01.begin()
+        s1.step(1)
+        d00.relay_b()
         s1.step(2)
 
-    staged(H, {0: lambda: s1.step(0), 1: before_chunk_1}, chunk_step)
-    d1.begin()
+    staged(4, {1: before_half_1, 2: before_half_2, 3: d10.begin}, half_step)
+    d11.begin()
     own_stats()
-    d0.end_b()
-
-    def send_weight(n, *then):
+    d00.end_b()
+
+    def weight_sent(n, *then):
         def action():
             start(weight_copies[n])
             for step in then:
@@ -454,7 +476,7 @@
 
         return action
 
-    def take_weight(n, *then):
+    def weight_came(n, *then):
         def action():
             arrive(weight_copies[n])
             for step in then:
@@ -462,13 +484,28 @@
 
         return action
 
-    staged(4, {1: send_weight(0), 2: send_weight(1, d1.relay_b), 3: send_weight(2)}, weight_other)
+    staged(4, {1: weight_sent(0, d01.end_b), 2: weight_sent(1, d10.relay_b), 3: weight_sent(2)}, weight_other)
     start(weight_copies[3])
-    d0.end_a()
-    staged(4, {0: take_weight(0), 1: take_weight(1, d1.end_b), 2: take_weight(2, d0.end_z),
-               3: take_weight(3, d1.end_a)}, weight_own)
+    d11.relay_b()
+
+    def before_own_1():
+        d00.end_a()
+        z0.send(0)
+        d10.end_b()
+
+    def before_own_2():
+        d01.end_a()
+        z0.send(1)
+
+    staged(4, {0: weight_came(0), 1: weight_came(1, before_own_1), 2: weight_came(2, before_own_2),
+               3: weight_came(3, d11.end_b)}, weight_own)
+    d10.end_a()
+    z1.send(0)
+    z0.end()
     own_stats_store()
-    d1.end_z()
+    d11.end_a()
+    z1.send(1)
+    z1.end()
     for copy in copies:
         copy.wait_send()
 
@@ -482,12 +519,12 @@
         pltpu.VMEM((NB, V, BLK), F32),
         pltpu.VMEM((NB, V, BLK), BF16),
         pltpu.VMEM((RING * BLK, V), BF16),
-        pltpu.VMEM((H, 4, HALF, D), F32),
-        pltpu.VMEM((H, 6, HALF, D), BF16),
-        pltpu.VMEM((H, 6, HALF, D), BF16),
-        pltpu.VMEM((H, 2, HALF, D), F32),
-        pltpu.VMEM((H, RING - 1, 2, R, D), BF16),
-        pltpu.VMEM((H, RING - 1, 2, R, D), BF16),
+        pltpu.VMEM((H, 2, 4, HALF, DC), F32),
+        pltpu.VMEM((H, 2, 6, HALF, DC), BF16),
+        pltpu.VMEM((H, 2, 6, HALF, DC), BF16),
+        pltpu.VMEM((H, 2, 2, HALF, DC), F32),
+        pltpu.VMEM((H, 2, RING - 1, 2, R, DC), BF16),
+        pltpu.VMEM((H, 2, RING - 1, 2, R, DC), BF16),
         pltpu.VMEM((H, NZ, 2, 2, R, 128), F32),
         pltpu.VMEM((H, 2, NZ, 2, R, 128), F32),
         pltpu.VMEM((NB, 4, BLK), F32),
@@ -524,10 +561,30 @@
     )(hid, w, ids, adv)
 
 
+def store_kernel(*refs):
+    count = len(refs) // 2
+    moves = [pltpu.make_async_copy(refs[i], refs[count + i], refs[-1].at[i]) for i in range(count)]
+    for move in moves:
+        move.start()
+    for move in moves:
+        move.wait()
+
+
+def store(*arrays):
+    return pl.pallas_call(
+        store_kernel,
+        out_shape=[jax.ShapeDtypeStruct(a.shape, a.dtype) for a in arrays],
+        in_specs=[pl.BlockSpec(memory_space=pltpu.VMEM)] * len(arrays),
+        out_specs=[pl.BlockSpec(memory_space=pl.ANY)] * len(arrays),
+        scratch_shapes=[pltpu.SemaphoreType.DMA((len(arrays),))],
+        compiler_params=pltpu.CompilerParams(vmem_limit_bytes=4 * 2**20),
+    )(*arrays)
+
+
 def shards(hidden, head_weight, sampled_ids, advantage):
     hid = hidden.reshape(2, H, 2, R, D)
-    grad_weight, grad_hidden, log_prob, entropy = call(
-        hid, head_weight, sampled_ids.reshape(16, 128), advantage.reshape(16, 128))
+    grad_weight, grad_hidden, log_prob, entropy = store(*call(
+        hid, head_weight, sampled_ids.reshape(16, 128), advantage.reshape(16, 128)))
     return (log_prob.reshape(SHARD), entropy.reshape(SHARD), grad_hidden.reshape(SHARD, 128), grad_weight)
 
 

time: 95.9 us -> 87.6 us (0.913)
  Pallas kernels: 91.5 us -> 86.9 us
  local copies, waits for them, and re-layouts: 3.67 us -> 0 us
    pallas_call x1, Pallas kernels: 91.5 us -> 84.8 us  [call(): pl.pallas_call(kernel, out_shape=(pltpu.VMEM((ROWS, D), F32), pltpu.VMEM(...]
    unnamed x4 -> x0, local copies, waits for them, and re-layouts: 3.67 us -> none
    pallas_call x0 -> x1, Pallas kernels: none -> 2.06 us  [store(): pl.pallas_call(store_kernel, out_shape=[jax.ShapeDtypeStruct(a.shape, a.d...]
where the time goes in v2:
time: 87.6 us; the launch traced here: 87.5 us
  Pallas kernels  86.9 us (99%)
    pallas_call x1, Pallas kernels, call(): pl.pallas_call(kernel, out_shape=(pltpu.VMEM((ROWS, D), F32), pltpu.VMEM(...  84.8 us
    pallas_call x1, Pallas kernels, store(): pl.pallas_call(store_kernel, out_shape=[jax.ShapeDtypeStruct(a.shape, a.d...  2.06 us

profile of v2, /device:TPU:1, one launch (start us, length us, event | category | flops | bytes accessed | tf_op | source)
XLA Modules:
  0.0 87.5 jit_solution(14738032084610139196)
XLA Ops:
  0.6 84.8 %shard_map.75 = (f32[512,2048]{1,0:T(8,128)S(1)}, f32[2,2,2,16,128]{4,3,2,1,0:T(8,128)S(1)}, f32[1,128]{1,0:T(1,128)S(1)}, f32[1,128]{1,0:T(1,128)S(1)}) custom-call(bf16[2,2,2,16,2048]{4,3,2,1,0:T(8,128)(2,1)} %bitcast.6, bf16[512,2048]{1,0:T(8,128)(2,1)} %w.1, s32[16,128]{1,0:T(8,128)} %bitcast.7, f32[16,128]{1,0:T(8,128)} %bitcast.8), custom_call_target="tpu_custom_call" | custom-call | tf_op jit(solution)/shard_map/pallas_call | solution.py:548
  85.5 2.1 %shard_map.76 = (f32[512,2048]{1,0:T(8,128)}, f32[2,2,2,16,128]{4,3,2,1,0:T(8,128)}, f32[1,128]{1,0:T(1,128)}, f32[1,128]{1,0:T(1,128)}) custom-call(f32[512,2048]{1,0:T(8,128)S(1)} %get-tuple-element.12.refs_0_, f32[2,2,2,16,128]{4,3,2,1,0:T(8,128)S(1)} %get-tuple-element.13.refs_1_, f32[1,128]{1,0:T(1,128)S(1)} %get-tuple-element.14.refs_2_, ...), custom_call_target="tpu_custom_call" | custom-call | tf_op jit(solution)/shard_map/pallas_call | solution.py:574

commit v3 on v2

--- a/solution.py
+++ b/solution.py
@@ -20,7 +20,7 @@
 BLK = 2 * RING * R
 HALF = RING * R
 NB = RING * H
-VC = 512
+VC = 256
 NC = 512
 DC = D // 2
 NSEM = 144
@@ -94,35 +94,24 @@
             self.near = [remote(own, there, d) for d in (ap, am)]
             self.far = [remote(hall.at[k0, 0, a_m], hall.at[k0, 0, a_m], ap),
                         remote(hall.at[k0, 1, a_p], hall.at[k0, 1, a_p], am)]
-            self.spread, self.pass_on = {}, {}
-            for slot, src in (("own", pa), ("m", a_m), ("p", a_p), ("2", a_2)):
-                ref = hall.at[k0, :, src]
-                self.spread[slot] = [remote(own if slot == "own" else ref, ref, d) for d in (bp, bm)]
-                one, two = hall.at[km, 0, src], hall.at[kp, 1, src]
-                self.pass_on[slot] = [remote(one, one, bp), remote(two, two, bm)]
+            halves = [hall.at[k0, s] for s in range(2)]
+            self.first = [remote(halves[0], halves[0], bp), remote(halves[1], halves[1], bm)]
+            self.second = [remote(halves[1], halves[1], bp), remote(halves[0], halves[0], bm)]
+            self.on = [remote(hall.at[km, 0], hall.at[km, 0], bp), remote(hall.at[kp, 1], hall.at[kp, 1], bm)]
 
         def ring(self):
             for near, far in zip(self.near, self.far):
                 arrive(near)
                 start(far)
 
-        def spread_on(self, *slots):
-            for slot in slots:
-                start(*self.spread[slot])
-
-        def ring_far(self):
+        def spread(self):
             arrive(*self.far)
-            start(*self.spread["2"])
-
-        def forward(self, *slots):
-            for slot in slots:
-                for came, on in zip(self.spread[slot], self.pass_on[slot]):
-                    arrive(came)
-                    start(on)
-
-        def last(self):
-            for on in self.pass_on.values():
-                arrive(*on)
+            start(*self.first, *self.second)
+
+        def pass_on(self):
+            for first, on in zip(self.first, self.on):
+                arrive(first)
+                start(on)
 
     g0, g1 = Gather(0), Gather(1)
 
@@ -150,32 +139,34 @@
     def stats_blocks(k_one, k_two):
         token_ids = jnp.concatenate([ids_row[k_one], ids_row[k_two]], axis=1) - first_row
 
-        def logits_step(v, peak):
-            rows = pl.ds(pl.multiple_of(v * VC, VC), VC)
+        def product(v):
             tokens = jnp.concatenate([hall[k_one].reshape(BLK, D), hall[k_two].reshape(BLK, D)], axis=0)
-            part = lax.dot_general(wall[rows, :], tokens, (((1,), (1,)), ((), ())), preferred_element_type=F32)
-            logits[k_one, rows, :] = part[:, :BLK]
-            logits[k_two, rows, :] = part[:, BLK:]
-            return jnp.maximum(peak, jnp.max(part.reshape(VC // 8, 8, 2 * BLK), axis=0))
-
-        peak = lax.fori_loop(0, V // VC, logits_step, jnp.full((8, 2 * BLK), -3e38, F32))
-        peak = jnp.max(peak, axis=0, keepdims=True)
-        step_rows = 256
-
-        def sums_step(v, sums):
-            start_row = pl.multiple_of(v * step_rows, step_rows)
-            rows = pl.ds(start_row, step_rows)
+            part = lax.dot_general(wall[v * VC:(v + 1) * VC, :], tokens, (((1,), (1,)), ((), ())),
+                                   preferred_element_type=F32)
+            logits[k_one, v * VC:(v + 1) * VC, :] = part[:, :BLK]
+            logits[k_two, v * VC:(v + 1) * VC, :] = part[:, BLK:]
+
+        def add_sums(v, peak, sums):
+            rows = slice(v * VC, (v + 1) * VC)
             part = jnp.concatenate([logits[k_one, rows, :], logits[k_two, rows, :]], axis=1)
-            expon = jnp.exp(part - peak)
+            above = jnp.max(part, axis=0, keepdims=True)
+            new_peak = above if peak is None else jnp.maximum(peak, above)
+            expon = jnp.exp(part - new_peak)
             row = lax.broadcasted_iota(jnp.int32, part.shape, 0)
-            picked = jnp.where(row == token_ids - start_row, part, 0.0)
-            return tuple(s + jnp.sum(p.reshape(step_rows // 8, 8, 2 * BLK), axis=0)
-                         for s, p in zip(sums, (expon, expon * part, picked)))
-
-        zero = jnp.zeros((8, 2 * BLK), F32)
-        sums = lax.fori_loop(0, V // step_rows, sums_step, (zero, zero, zero))
-        sums = tuple(jnp.sum(s, axis=0, keepdims=True) for s in sums)
-        for q, row in enumerate((peak,) + sums):
+            picked = jnp.where(row == token_ids - v * VC, part, 0.0)
+            more = [jnp.sum(p, axis=0, keepdims=True) for p in (expon, expon * part, picked)]
+            if peak is not None:
+                scale = jnp.exp(peak - new_peak)
+                more = [m + s * f for m, s, f in zip(more, sums, (scale, scale, 1.0))]
+            return new_peak, more
+
+        peak, sums = None, None
+        product(0)
+        for v in range(1, V // VC):
+            product(v)
+            peak, sums = add_sums(v - 1, peak, sums)
+        peak, sums = add_sums(V // VC - 1, peak, sums)
+        for q, row in enumerate([peak] + sums):
             st[k_one, pl.ds(q, 1), :] = row[:, :BLK]
             st[k_two, pl.ds(q, 1), :] = row[:, BLK:]
 
@@ -226,6 +217,7 @@
         advantage = jnp.concatenate([adv_row[k] for k in ks], axis=1)
         log_total = jnp.concatenate([fin[2, k, 0:1, :] for k in ks], axis=1)
         mean = jnp.concatenate([fin[2, k, 1:2, :] for k in ks], axis=1)
+        level = advantage - ENTROPY_COEF * mean
         step_rows = 128
 
         def grad_step(v, carry):
@@ -234,8 +226,8 @@
             part = jnp.concatenate([logits[k, rows, :] for k in ks], axis=1)
             prob = jnp.exp(part - log_total)
             row = lax.broadcasted_iota(jnp.int32, part.shape, 0)
-            onehot = jnp.where(row == token_ids - start_row, 1.0, 0.0)
-            low = (advantage * (onehot - prob) - ENTROPY_COEF * prob * (part - mean)).astype(BF16)
+            chosen = jnp.where(row == token_ids - start_row, advantage, 0.0)
+            low = (chosen - prob * (level + ENTROPY_COEF * part)).astype(BF16)
             for j, k in enumerate(ks):
                 tile = low[:, j * BLK:(j + 1) * BLK]
                 grad[k, rows, :] = tile
@@ -252,10 +244,10 @@
                            preferred_element_type=F32)
             two_0, two_1, m_0, m_1, p_0, p_1, own_0, own_1 = (part[i * HALF:(i + 1) * HALF] for i in range(8))
             x1[h, c, 0, :, cols] = two_0.astype(BF16)
-            x1[h, c, 1, :, cols] = two_1.astype(BF16)
+            x1[h, c, 1, :, cols] = m_1.astype(BF16)
+            x1[h, c, 2, :, cols] = two_1.astype(BF16)
+            x1[h, c, 3, :, cols] = p_0.astype(BF16)
             pm[h, c, 0, :, cols] = m_0
-            x1[h, c, 2, :, cols] = m_1.astype(BF16)
-            x1[h, c, 3, :, cols] = p_0.astype(BF16)
             pm[h, c, 1, :, cols] = p_1
             pm[h, c, 2, :, cols] = own_0
             pm[h, c, 3, :, cols] = own_1
@@ -265,10 +257,10 @@
 
     def chunked(rows, body):
         def step(n, carry):
-            body(pl.ds(pl.multiple_of(n * 16, 16), 16))
+            body(pl.ds(pl.multiple_of(n * 32, 32), 32))
             return carry
 
-        lax.fori_loop(0, rows // 16, step, 0)
+        lax.fori_loop(0, rows // 32, step, 0)
 
     def slot(a):
         return pl.ds(pl.multiple_of(a * R, R), R)
@@ -276,11 +268,12 @@
     class Reduce:
         def __init__(self, h, c):
             self.at = h, c
-            self.b = [remote(x1.at[h, c, i], y1.at[h, c, i], d) for i, d in enumerate((bm, bp, bm, bp, bm, bp))]
+            self.b = [remote(x1.at[h, c, i:i + 2], y1.at[h, c, i:i + 2], d) for i, d in ((0, bm), (2, bp))]
+            self.b += [remote(x1.at[h, c, i], y1.at[h, c, i], d) for i, d in ((4, bm), (5, bp))]
             self.a = [remote(x2.at[h, c, i], y2.at[h, c, i], d) for i, d in enumerate(a_dev)]
 
         def begin(self):
-            start(*self.b[:4])
+            start(*self.b[:2])
 
         def relay_b(self):
             h, c = self.at
@@ -289,15 +282,15 @@
 
                 def relay(rows):
                     x1[h, c, 4 + i, rows, :] = (
-                        pm[h, c, i, rows, :] + y1[h, c, i, rows, :].astype(F32)).astype(BF16)
+                        pm[h, c, i, rows, :] + y1[h, c, 2 * i, rows, :].astype(F32)).astype(BF16)
 
                 chunked(HALF, relay)
-                start(self.b[4 + i])
+                start(self.b[2 + i])
 
         def end_b(self):
             h, c = self.at
             arrive(*self.b[2:])
-            for s, (one, two) in enumerate(((3, 4), (2, 5))):
+            for s, (one, two) in enumerate(((3, 4), (1, 5))):
 
                 def total(rows):
                     r1[h, c, s, rows, :] = (pm[h, c, 2 + s, rows, :] + y1[h, c, one, rows, :].astype(F32)
@@ -405,19 +398,16 @@
     reorder(ids_in, ids_row)
     reorder(adv_in, adv_row)
     pl.semaphore_wait(barrier, len(peers))
-    start(*g0.near, *g0.spread["own"], *g1.near)
+    start(*g0.near, *g1.near)
     for c in [w_in] + own_in:
         c.wait()
     start(w_swap)
     g0.ring()
-    g0.spread_on("m", "p")
-    g0.forward("own")
-    g0.ring_far()
-    g0.forward("m", "p", "2")
-    g1.spread_on("own")
     g1.ring()
-    g1.spread_on("m", "p")
-    arrive(w_swap)
+    g0.spread()
+    g0.pass_on()
+    g1.spread()
+    arrive(w_swap, *g0.second)
 
     def unit(i):
         half = lax.rem(i, 2)
@@ -425,19 +415,17 @@
         stats_blocks(k + lax.rem(pb + half, RING), k + lax.rem(pb + 3 - half, RING))
 
     def before_1():
-        g1.forward("own")
-        g0.last()
+        arrive(*g0.on)
 
     def before_2():
         s0.begin()
-        g1.ring_far()
-        g1.forward("m", "p")
+        g1.pass_on()
         s0.step(0)
-        g1.forward("2")
+        arrive(*g1.second)
 
     def before_3():
         s0.step(1)
-        g1.last()
+        arrive(*g1.on)
 
     staged(4, {1: before_1, 2: before_2, 3: before_3}, unit)
     s1.begin()
@@ -505,8 +493,12 @@
     own_stats_store()
     d11.end_a()
     z1.send(1)
+    last = [z1.sibling] + [copy for both in z1.others for copy in both]
+    for copy in copies:
+        if not any(copy is other for other in last):
+            copy.wait_send()
     z1.end()
-    for copy in copies:
+    for copy in last:
         copy.wait_send()
 
 

time: 87.6 us -> 86.9 us (level)
  no operation moved by 1% of the time
where the time goes in v3:
time: 86.9 us; the launch traced here: 86.8 us
  Pallas kernels  86.2 us (99%)
    pallas_call x1, Pallas kernels, call(): pl.pallas_call(kernel, out_shape=(pltpu.VMEM((ROWS, D), F32), pltpu.VMEM(...  84.1 us
    pallas_call x1, Pallas kernels, store(): pl.pallas_call(store_kernel, out_shape=[jax.ShapeDtypeStruct(a.shape, a.d...  2.06 us

profile of v3, /device:TPU:1, one launch (start us, length us, event | category | flops | bytes accessed | tf_op | source)
XLA Modules:
  0.0 86.8 jit_solution(18421924800996309114)
XLA Ops:
  0.6 84.1 %shard_map.75 = (f32[512,2048]{1,0:T(8,128)S(1)}, f32[2,2,2,16,128]{4,3,2,1,0:T(8,128)S(1)}, f32[1,128]{1,0:T(1,128)S(1)}, f32[1,128]{1,0:T(1,128)S(1)}) custom-call(bf16[2,2,2,16,2048]{4,3,2,1,0:T(8,128)(2,1)} %bitcast.6, bf16[512,2048]{1,0:T(8,128)(2,1)} %w.1, s32[16,128]{1,0:T(8,128)} %bitcast.7, f32[16,128]{1,0:T(8,128)} %bitcast.8), custom_call_target="tpu_custom_call" | custom-call | tf_op jit(solution)/shard_map/pallas_call | solution.py:540
  84.8 2.1 %shard_map.76 = (f32[512,2048]{1,0:T(8,128)}, f32[2,2,2,16,128]{4,3,2,1,0:T(8,128)}, f32[1,128]{1,0:T(1,128)}, f32[1,128]{1,0:T(1,128)}) custom-call(f32[512,2048]{1,0:T(8,128)S(1)} %get-tuple-element.12.refs_0_, f32[2,2,2,16,128]{4,3,2,1,0:T(8,128)S(1)} %get-tuple-element.13.refs_1_, f32[1,128]{1,0:T(1,128)S(1)} %get-tuple-element.14.refs_2_, ...), custom_call_target="tpu_custom_call" | custom-call | tf_op jit(solution)/shard_map/pallas_call | solution.py:566

commit v4 on v3

--- a/solution.py
+++ b/solution.py
@@ -105,7 +105,6 @@
                 start(far)
 
         def spread(self):
-            arrive(*self.far)
             start(*self.first, *self.second)
 
         def pass_on(self):
@@ -136,19 +135,19 @@
 
     first_row = dp * (2 * ROWS * NZ) + z * (2 * ROWS)
 
-    def stats_blocks(k_one, k_two):
-        token_ids = jnp.concatenate([ids_row[k_one], ids_row[k_two]], axis=1) - first_row
+    def stats_blocks(*ks):
+        token_ids = jnp.concatenate([ids_row[k] for k in ks], axis=1) - first_row
 
         def product(v):
-            tokens = jnp.concatenate([hall[k_one].reshape(BLK, D), hall[k_two].reshape(BLK, D)], axis=0)
+            tokens = jnp.concatenate([hall[k].reshape(BLK, D) for k in ks], axis=0)
             part = lax.dot_general(wall[v * VC:(v + 1) * VC, :], tokens, (((1,), (1,)), ((), ())),
                                    preferred_element_type=F32)
-            logits[k_one, v * VC:(v + 1) * VC, :] = part[:, :BLK]
-            logits[k_two, v * VC:(v + 1) * VC, :] = part[:, BLK:]
+            for j, k in enumerate(ks):
+                logits[k, v * VC:(v + 1) * VC, :] = part[:, j * BLK:(j + 1) * BLK]
 
         def add_sums(v, peak, sums):
             rows = slice(v * VC, (v + 1) * VC)
-            part = jnp.concatenate([logits[k_one, rows, :], logits[k_two, rows, :]], axis=1)
+            part = jnp.concatenate([logits[k, rows, :] for k in ks], axis=1)
             above = jnp.max(part, axis=0, keepdims=True)
             new_peak = above if peak is None else jnp.maximum(peak, above)
             expon = jnp.exp(part - new_peak)
@@ -167,8 +166,8 @@
             peak, sums = add_sums(v - 1, peak, sums)
         peak, sums = add_sums(V // VC - 1, peak, sums)
         for q, row in enumerate([peak] + sums):
-            st[k_one, pl.ds(q, 1), :] = row[:, :BLK]
-            st[k_two, pl.ds(q, 1), :] = row[:, BLK:]
+            for j, k in enumerate(ks):
+                st[k, pl.ds(q, 1), :] = row[:, j * BLK:(j + 1) * BLK]
 
     def stats_merge(ref, slots, sent):
         arrive(*sent)
@@ -238,10 +237,9 @@
 
     def product_half(h, c):
         def product_step(n, carry):
-            start_col = pl.multiple_of(n * NC, NC)
-            cols = pl.ds(start_col, NC)
-            part = jnp.dot(grad_t[...], wall[:, pl.ds(pl.multiple_of(c * DC + start_col, NC), NC)],
-                           preferred_element_type=F32)
+            cols = pl.ds(pl.multiple_of(n * NC, NC), NC)
+            rhs = [wall[:, pl.ds(pl.multiple_of((n * (NC // 128) + j) * 256 + c * 128, 128), 128)] for j in range(NC // 128)]
+            part = jnp.dot(grad_t[...], jnp.concatenate(rhs, axis=1), preferred_element_type=F32)
             two_0, two_1, m_0, m_1, p_0, p_1, own_0, own_1 = (part[i * HALF:(i + 1) * HALF] for i in range(8))
             x1[h, c, 0, :, cols] = two_0.astype(BF16)
             x1[h, c, 1, :, cols] = m_1.astype(BF16)
@@ -306,9 +304,9 @@
             h, c = self.at
             arrive(*self.a)
             for s in range(2):
-                for f in range(DC // 128):
-                    cols = slice(f * 128, f * 128 + 128)
-                    zs[h, c * (NZ // 2) + f // 2, f % 2, s] = r1[h, c, s, slot(pa), cols] + sum(
+                for j in range(NZ):
+                    cols = slice(j * 128, j * 128 + 128)
+                    zs[h, j, c, s] = r1[h, c, s, slot(pa), cols] + sum(
                         y2[h, c, i, s, :, cols].astype(F32) for i in range(RING - 1))
 
     class Reduce_z:
@@ -323,16 +321,15 @@
                 device_id=sibling, device_id_type=MESH) for c, k in places]
 
         def send(self, c):
-            @pl.when(lax.div(z, NZ // 2) == c)
+            start(*[both[c] for both in self.others])
+
+            @pl.when(core == c)
             def _():
                 zr[self.h, core, 0] = zs[self.h, z, core]
+
+            @pl.when(core != c)
+            def _():
                 start(self.sibling)
-
-            for k in range(1, NZ):
-
-                @pl.when(lax.div(lax.rem(z + k, NZ), NZ // 2) == c)
-                def _():
-                    start(*self.others[k - 1])
 
         def end(self):
             h = self.h
@@ -393,42 +390,32 @@
 
         lax.fori_loop(0, count, step, 0)
 
-    for c in small_in:
+    pl.semaphore_wait(barrier, len(peers))
+    start(*g0.near, *g1.near)
+    w_in.wait()
+    start(w_swap)
+    for c in small_in + own_in:
         c.wait()
     reorder(ids_in, ids_row)
     reorder(adv_in, adv_row)
-    pl.semaphore_wait(barrier, len(peers))
-    start(*g0.near, *g1.near)
-    for c in [w_in] + own_in:
-        c.wait()
-    start(w_swap)
     g0.ring()
     g1.ring()
+    arrive(*g0.far)
     g0.spread()
+    arrive(*g1.far, w_swap)
+    stats_blocks(pb, RING + pb)
     g0.pass_on()
     g1.spread()
-    arrive(w_swap, *g0.second)
-
-    def unit(i):
-        half = lax.rem(i, 2)
-        k = lax.div(i, 2) * RING
-        stats_blocks(k + lax.rem(pb + half, RING), k + lax.rem(pb + 3 - half, RING))
-
-    def before_1():
-        arrive(*g0.on)
-
-    def before_2():
-        s0.begin()
-        g1.pass_on()
-        s0.step(0)
-        arrive(*g1.second)
-
-    def before_3():
-        s0.step(1)
-        arrive(*g1.on)
-
-    staged(4, {1: before_1, 2: before_2, 3: before_3}, unit)
-    s1.begin()
+    arrive(*g0.second)
+    stats_blocks(b_m, b_p)
+    arrive(*g0.on)
+    stats_blocks(b_2)
+    s0.begin()
+    g1.pass_on()
+    s0.step(0)
+    s0.step(1)
+    arrive(*g1.second)
+    stats_blocks(RING + b_m, RING + b_p)
     s0.step(2)
 
     def half_step(i):
@@ -438,23 +425,30 @@
         def _():
             grad_chunk(h)
 
-        pl.when(i == 2)(d01.relay_b)
+        pl.when(i == 2)(d00.end_b)
         product_half(h, c)
 
     def before_half_1():
         d00.begin()
-        s1.step(0)
+        arrive(*g1.on)
+        stats_blocks(RING + b_2)
+        s1.begin()
 
     def before_half_2():
         d01.begin()
+        s1.step(0)
+        d00.relay_b()
         s1.step(1)
-        d00.relay_b()
+        d01.relay_b()
         s1.step(2)
 
-    staged(4, {1: before_half_1, 2: before_half_2, 3: d10.begin}, half_step)
+    def before_half_3():
+        d10.begin()
+        d01.end_b()
+
+    staged(4, {1: before_half_1, 2: before_half_2, 3: before_half_3}, half_step)
     d11.begin()
     own_stats()
-    d00.end_b()
 
     def weight_sent(n, *then):
         def action():
@@ -472,25 +466,21 @@
 
         return action
 
-    staged(4, {1: weight_sent(0, d01.end_b), 2: weight_sent(1, d10.relay_b), 3: weight_sent(2)}, weight_other)
-    start(weight_copies[3])
-    d11.relay_b()
-
-    def before_own_1():
+    def z0_first():
         d00.end_a()
         z0.send(0)
-        d10.end_b()
-
-    def before_own_2():
-        d01.end_a()
-        z0.send(1)
-
-    staged(4, {0: weight_came(0), 1: weight_came(1, before_own_1), 2: weight_came(2, before_own_2),
-               3: weight_came(3, d11.end_b)}, weight_own)
+
+    staged(4, {1: weight_sent(0), 2: weight_sent(1, z0_first), 3: weight_sent(2, d10.relay_b)}, weight_other)
+    start(weight_copies[3])
+    d01.end_a()
+    z0.send(1)
+    staged(4, {0: weight_came(0), 1: weight_came(1), 2: weight_came(2, d11.relay_b), 3: weight_came(3)}, weight_own)
+    d10.end_b()
+    z0.end()
+    own_stats_store()
+    d11.end_b()
     d10.end_a()
     z1.send(0)
-    z0.end()
-    own_stats_store()
     d11.end_a()
     z1.send(1)
     last = [z1.sibling] + [copy for both in z1.others for copy in both]

time: 86.9 us -> 94.3 us (1.085)
  Pallas kernels: 86.2 us -> 93.6 us
    pallas_call x1, Pallas kernels: 84.1 us -> 91.5 us  [call(): pl.pallas_call(kernel, out_shape=(pltpu.VMEM((ROWS, D), F32), pltpu.VMEM(...]
where the time goes in v4:
time: 94.3 us; the launch traced here: 94.2 us
  Pallas kernels  93.6 us (99%)
    pallas_call x1, Pallas kernels, call(): pl.pallas_call(kernel, out_shape=(pltpu.VMEM((ROWS, D), F32), pltpu.VMEM(...  91.5 us
    pallas_call x1, Pallas kernels, store(): pl.pallas_call(store_kernel, out_shape=[jax.ShapeDtypeStruct(a.shape, a.d...  2.06 us

profile of v4, /device:TPU:1, one launch (start us, length us, event | category | flops | bytes accessed | tf_op | source)
XLA Modules:
  0.0 94.2 jit_solution(11619915370874972313)
XLA Ops:
  0.6 91.5 %shard_map.75 = (f32[512,2048]{1,0:T(8,128)S(1)}, f32[2,2,2,16,128]{4,3,2,1,0:T(8,128)S(1)}, f32[1,128]{1,0:T(1,128)S(1)}, f32[1,128]{1,0:T(1,128)S(1)}) custom-call(bf16[2,2,2,16,2048]{4,3,2,1,0:T(8,128)(2,1)} %bitcast.6, bf16[512,2048]{1,0:T(8,128)(2,1)} %w.1, s32[16,128]{1,0:T(8,128)} %bitcast.7, f32[16,128]{1,0:T(8,128)} %bitcast.8), custom_call_target="tpu_custom_call" | custom-call | tf_op jit(solution)/shard_map/pallas_call | solution.py:530
  92.1 2.1 %shard_map.76 = (f32[512,2048]{1,0:T(8,128)}, f32[2,2,2,16,128]{4,3,2,1,0:T(8,128)}, f32[1,128]{1,0:T(1,128)}, f32[1,128]{1,0:T(1,128)}) custom-call(f32[512,2048]{1,0:T(8,128)S(1)} %get-tuple-element.12.refs_0_, f32[2,2,2,16,128]{4,3,2,1,0:T(8,128)S(1)} %get-tuple-element.13.refs_1_, f32[1,128]{1,0:T(1,128)S(1)} %get-tuple-element.14.refs_2_, ...), custom_call_target="tpu_custom_call" | custom-call | tf_op jit(solution)/shard_map/pallas_call | solution.py:556

commit v5 on v3

--- a/solution.py
+++ b/solution.py
@@ -210,50 +210,51 @@
     s0, s1 = Stats(0), Stats(1)
 
     order = (b_2, b_m, b_p, pb)
-
-    def grad_chunk(h):
-        ks = [h * RING + b for b in order]
+    STEPS = D // NC
+    GR = V // STEPS
+
+    def grad_step(h, pair, v):
+        ks = [h * RING + b for b in order[2 * pair:2 * pair + 2]]
         token_ids = jnp.concatenate([ids_row[k] for k in ks], axis=1) - first_row
         advantage = jnp.concatenate([adv_row[k] for k in ks], axis=1)
         log_total = jnp.concatenate([fin[2, k, 0:1, :] for k in ks], axis=1)
         mean = jnp.concatenate([fin[2, k, 1:2, :] for k in ks], axis=1)
         level = advantage - ENTROPY_COEF * mean
-        step_rows = 128
-
-        def grad_step(v, carry):
-            start_row = pl.multiple_of(v * step_rows, step_rows)
-            rows = pl.ds(start_row, step_rows)
-            part = jnp.concatenate([logits[k, rows, :] for k in ks], axis=1)
-            prob = jnp.exp(part - log_total)
-            row = lax.broadcasted_iota(jnp.int32, part.shape, 0)
-            chosen = jnp.where(row == token_ids - start_row, advantage, 0.0)
-            low = (chosen - prob * (level + ENTROPY_COEF * part)).astype(BF16)
-            for j, k in enumerate(ks):
-                tile = low[:, j * BLK:(j + 1) * BLK]
-                grad[k, rows, :] = tile
-                grad_t[j * BLK:(j + 1) * BLK, rows] = tile.T
+        start_row = pl.multiple_of(v * GR, GR)
+        rows = pl.ds(start_row, GR)
+        part = jnp.concatenate([logits[k, rows, :] for k in ks], axis=1)
+        prob = jnp.exp(part - log_total)
+        row = lax.broadcasted_iota(jnp.int32, part.shape, 0)
+        chosen = jnp.where(row == token_ids - start_row, advantage, 0.0)
+        low = (chosen - prob * (level + ENTROPY_COEF * part)).astype(BF16)
+        for j, k in enumerate(ks):
+            tile = low[:, j * BLK:(j + 1) * BLK]
+            grad[k, rows, :] = tile
+            grad_t[pair, j * BLK:(j + 1) * BLK, rows] = tile.T
+
+    def product_step(h, pair, n):
+        c, m = lax.div(n, STEPS // 2), lax.rem(n, STEPS // 2)
+        cols = pl.ds(pl.multiple_of(m * NC, NC), NC)
+        part = jnp.dot(grad_t[pair], wall[:, pl.ds(pl.multiple_of(n * NC, NC), NC)], preferred_element_type=F32)
+        one_0, one_1, two_0, two_1 = (part[i * HALF:(i + 1) * HALF] for i in range(4))
+        if pair == 0:
+            x1[h, c, 0, :, cols] = one_0.astype(BF16)
+            x1[h, c, 2, :, cols] = one_1.astype(BF16)
+            pm[h, c, 0, :, cols] = two_0
+            x1[h, c, 1, :, cols] = two_1.astype(BF16)
+        else:
+            x1[h, c, 3, :, cols] = one_0.astype(BF16)
+            pm[h, c, 1, :, cols] = one_1
+            pm[h, c, 2, :, cols] = two_0
+            pm[h, c, 3, :, cols] = two_1
+
+    def each_step(*bodies):
+        def step(n, carry):
+            for body in bodies:
+                body(n)
             return carry
 
-        lax.fori_loop(0, V // step_rows, grad_step, 0)
-
-    def product_half(h, c):
-        def product_step(n, carry):
-            start_col = pl.multiple_of(n * NC, NC)
-            cols = pl.ds(start_col, NC)
-            part = jnp.dot(grad_t[...], wall[:, pl.ds(pl.multiple_of(c * DC + start_col, NC), NC)],
-                           preferred_element_type=F32)
-            two_0, two_1, m_0, m_1, p_0, p_1, own_0, own_1 = (part[i * HALF:(i + 1) * HALF] for i in range(8))
-            x1[h, c, 0, :, cols] = two_0.astype(BF16)
-            x1[h, c, 1, :, cols] = m_1.astype(BF16)
-            x1[h, c, 2, :, cols] = two_1.astype(BF16)
-            x1[h, c, 3, :, cols] = p_0.astype(BF16)
-            pm[h, c, 0, :, cols] = m_0
-            pm[h, c, 1, :, cols] = p_1
-            pm[h, c, 2, :, cols] = own_0
-            pm[h, c, 3, :, cols] = own_1
-            return carry
-
-        lax.fori_loop(0, DC // NC, product_step, 0)
+        lax.fori_loop(0, STEPS, step, 0)
 
     def chunked(rows, body):
         def step(n, carry):
@@ -268,12 +269,12 @@
     class Reduce:
         def __init__(self, h, c):
             self.at = h, c
-            self.b = [remote(x1.at[h, c, i:i + 2], y1.at[h, c, i:i + 2], d) for i, d in ((0, bm), (2, bp))]
-            self.b += [remote(x1.at[h, c, i], y1.at[h, c, i], d) for i, d in ((4, bm), (5, bp))]
+            self.b = [remote(x1.at[h, c, i], y1.at[h, c, i], d)
+                      for i, d in ((0, bm), (2, bp), (1, bm), (3, bp), (4, bm), (5, bp))]
             self.a = [remote(x2.at[h, c, i], y2.at[h, c, i], d) for i, d in enumerate(a_dev)]
 
-        def begin(self):
-            start(*self.b[:2])
+        def send(self, *which):
+            start(*[self.b[i] for i in which])
 
         def relay_b(self):
             h, c = self.at
@@ -285,7 +286,7 @@
                         pm[h, c, i, rows, :] + y1[h, c, 2 * i, rows, :].astype(F32)).astype(BF16)
 
                 chunked(HALF, relay)
-                start(self.b[2 + i])
+                start(self.b[4 + i])
 
         def end_b(self):
             h, c = self.at
@@ -431,30 +432,40 @@
     s1.begin()
     s0.step(2)
 
-    def half_step(i):
-        h, c = lax.div(i, 2), lax.rem(i, 2)
-
-        @pl.when(c == 0)
+    def chunk_step(h):
+        each_step(lambda v: grad_step(h, 0, v))
+        pl.when(h == 1)(d01.relay_b)
+        each_step(lambda n: product_step(h, 0, n), lambda v: grad_step(h, 1, v))
+
+        @pl.when(h == 0)
         def _():
-            grad_chunk(h)
-
-        pl.when(i == 2)(d01.relay_b)
-        product_half(h, c)
-
-    def before_half_1():
-        d00.begin()
-        s1.step(0)
-
-    def before_half_2():
-        d01.begin()
+            d00.send(0, 1)
+            d01.send(0, 1)
+            d00.send(2)
+            d01.send(2)
+            s1.step(0)
+
+        @pl.when(h == 1)
+        def _():
+            d10.send(0, 1)
+            d11.send(0, 1)
+            d10.send(2)
+            d11.send(2)
+            d00.end_b()
+
+        each_step(lambda n: product_step(h, 1, n))
+
+    def before_chunk_1():
+        d00.send(3)
+        d01.send(3)
         s1.step(1)
         d00.relay_b()
         s1.step(2)
 
-    staged(4, {1: before_half_1, 2: before_half_2, 3: d10.begin}, half_step)
-    d11.begin()
+    staged(H, {1: before_chunk_1}, chunk_step)
+    d10.send(3)
+    d11.send(3)
     own_stats()
-    d00.end_b()
 
     def weight_sent(n, *then):
         def action():
@@ -510,7 +521,7 @@
         pltpu.VMEM((V, D), BF16),
         pltpu.VMEM((NB, V, BLK), F32),
         pltpu.VMEM((NB, V, BLK), BF16),
-        pltpu.VMEM((RING * BLK, V), BF16),
+        pltpu.VMEM((2, 2 * BLK, V), BF16),
         pltpu.VMEM((H, 2, 4, HALF, DC), F32),
         pltpu.VMEM((H, 2, 6, HALF, DC), BF16),
         pltpu.VMEM((H, 2, 6, HALF, DC), BF16),

time: 86.9 us -> 86 us (0.990)
  Pallas kernels: 86.2 us -> 85.3 us
    pallas_call x1, Pallas kernels: 84.1 us -> 83.2 us  [call(): pl.pallas_call(kernel, out_shape=(pltpu.VMEM((ROWS, D), F32), pltpu.VMEM(...]
where the time goes in v5:
time: 86 us; the launch traced here: 85.9 us
  Pallas kernels  85.3 us (99%)
    pallas_call x1, Pallas kernels, call(): pl.pallas_call(kernel, out_shape=(pltpu.VMEM((ROWS, D), F32), pltpu.VMEM(...  83.2 us
    pallas_call x1, Pallas kernels, store(): pl.pallas_call(store_kernel, out_shape=[jax.ShapeDtypeStruct(a.shape, a.d...  2.06 us

profile of v5, /device:TPU:1, one launch (start us, length us, event | category | flops | bytes accessed | tf_op | source)
XLA Modules:
  0.0 85.9 jit_solution(6784725555048138723)
XLA Ops:
  0.6 83.2 %shard_map.75 = (f32[512,2048]{1,0:T(8,128)S(1)}, f32[2,2,2,16,128]{4,3,2,1,0:T(8,128)S(1)}, f32[1,128]{1,0:T(1,128)S(1)}, f32[1,128]{1,0:T(1,128)S(1)}) custom-call(bf16[2,2,2,16,2048]{4,3,2,1,0:T(8,128)(2,1)} %bitcast.6, bf16[512,2048]{1,0:T(8,128)(2,1)} %w.1, s32[16,128]{1,0:T(8,128)} %bitcast.7, f32[16,128]{1,0:T(8,128)} %bitcast.8), custom_call_target="tpu_custom_call" | custom-call | tf_op jit(solution)/shard_map/pallas_call | solution.py:551
  83.9 2.1 %shard_map.76 = (f32[512,2048]{1,0:T(8,128)}, f32[2,2,2,16,128]{4,3,2,1,0:T(8,128)}, f32[1,128]{1,0:T(1,128)}, f32[1,128]{1,0:T(1,128)}) custom-call(f32[512,2048]{1,0:T(8,128)S(1)} %get-tuple-element.12.refs_0_, f32[2,2,2,16,128]{4,3,2,1,0:T(8,128)S(1)} %get-tuple-element.13.refs_1_, f32[1,128]{1,0:T(1,128)S(1)} %get-tuple-element.14.refs_2_, ...), custom_call_target="tpu_custom_call" | custom-call | tf_op jit(solution)/shard_map/pallas_call | solution.py:577

commit v6 on v5

--- a/solution.py
+++ b/solution.py
@@ -27,8 +27,8 @@
 
 
 def kernel(hid, w, ids, adv, gw_out, gh_out, lp_out, en_out,
-           hall, wall, logits, grad, grad_t, pm, x1, y1, r1, x2, y2, zs, zr, st, sx, sy, sz, fin,
-           ids_in, adv_in, rolled, ids_row, adv_row, stat_swap, gw_send, gw_recv, send_sem, recv_sem, z_sem, local_sem):
+           hall, wall, logits, grad, grad_t, pm, x1, y1, yz, r1, x2, y2, zs, zr, st, sx, sy, sz, fin,
+           ids_in, adv_in, rolled, ids_row, adv_row, stat_swap, gw_send, gw_recv, send_sem, recv_sem, z_sem, pass_sem, local_sem):
     dp, vo = lax.axis_index("dp"), lax.axis_index("vocab")
     x, y = lax.div(dp, RING), lax.rem(dp, RING)
     z, core = lax.div(vo, 2), lax.rem(vo, 2)
@@ -241,10 +241,12 @@
             x1[h, c, 0, :, cols] = one_0.astype(BF16)
             x1[h, c, 2, :, cols] = one_1.astype(BF16)
             pm[h, c, 0, :, cols] = two_0
+            x1[h, c, 4, :, cols] = two_0.astype(BF16)
             x1[h, c, 1, :, cols] = two_1.astype(BF16)
         else:
             x1[h, c, 3, :, cols] = one_0.astype(BF16)
             pm[h, c, 1, :, cols] = one_1
+            x1[h, c, 5, :, cols] = one_1.astype(BF16)
             pm[h, c, 2, :, cols] = two_0
             pm[h, c, 3, :, cols] = two_1
 
@@ -269,28 +271,15 @@
     class Reduce:
         def __init__(self, h, c):
             self.at = h, c
-            self.b = [remote(x1.at[h, c, i], y1.at[h, c, i], d)
-                      for i, d in ((0, bm), (2, bp), (1, bm), (3, bp), (4, bm), (5, bp))]
+            self.direct = [remote(x1.at[h, c, i], y1.at[h, c, i], d) for i, d in ((1, bm), (3, bp))]
+            self.passed = [pltpu.make_async_remote_copy(
+                src_ref=x1.at[h, c, 4 + i], dst_ref=y1.at[h, c, 4 + i], send_sem=send_sem.at[0],
+                recv_sem=pass_sem.at[h, c, i], device_id=d, device_id_type=MESH) for i, d in enumerate((bm, bp))]
             self.a = [remote(x2.at[h, c, i], y2.at[h, c, i], d) for i, d in enumerate(a_dev)]
-
-        def send(self, *which):
-            start(*[self.b[i] for i in which])
-
-        def relay_b(self):
-            h, c = self.at
-            for i in range(2):
-                arrive(self.b[i])
-
-                def relay(rows):
-                    x1[h, c, 4 + i, rows, :] = (
-                        pm[h, c, i, rows, :] + y1[h, c, 2 * i, rows, :].astype(F32)).astype(BF16)
-
-                chunked(HALF, relay)
-                start(self.b[4 + i])
 
         def end_b(self):
             h, c = self.at
-            arrive(*self.b[2:])
+            arrive(*self.direct, *self.passed)
             for s, (one, two) in enumerate(((3, 4), (1, 5))):
 
                 def total(rows):
@@ -344,6 +333,42 @@
                     total += zr[h, c, k]
                 gh_out[c, h] = total
 
+    kept = lax.rem(z, 2)
+
+    class Far:
+        def __init__(self, h):
+            self.h = h
+            self.swap = [remote(x1.at[h, 1 - kept, 0], yz.at[h, 0], zdev(1)),
+                         remote(x1.at[h, 1 - kept, 2], yz.at[h, 1], zdev(NZ - 1))]
+            self.far = [remote(x1.at[h, kept, 2 * i], y1.at[h, kept, 2 * i], d) for i, d in enumerate((bm, bp))]
+            self.own, self.relayed = ([remote(x1.at[h, half, 4 + i], y1.at[h, half, 4 + i], d, pass_sem.at[h, half, i])
+                                       for i, d in enumerate((bm, bp))] for half in (1 - kept, kept))
+
+        def send(self):
+            h = self.h
+            for i in range(2):
+                arrive(self.swap[i])
+
+                def add(rows):
+                    x1[h, kept, 2 * i, rows, :] = (
+                        x1[h, kept, 2 * i, rows, :].astype(F32) + yz[h, i, rows, :].astype(F32)).astype(BF16)
+
+                chunked(HALF, add)
+                start(self.far[i])
+
+        def relay(self):
+            h = self.h
+            for i in range(2):
+                arrive(self.far[i])
+
+                def add(rows):
+                    x1[h, kept, 4 + i, rows, :] = (
+                        pm[h, kept, i, rows, :] + y1[h, kept, 2 * i, rows, :].astype(F32)).astype(BF16)
+
+                chunked(HALF, add)
+                start(self.relayed[i])
+
+    f0, f1 = Far(0), Far(1)
     d00, d01, d10, d11 = (Reduce(h, c) for h in range(H) for c in range(2))
     z0, z1 = Reduce_z(0), Reduce_z(1)
 
@@ -434,37 +459,30 @@
 
     def chunk_step(h):
         each_step(lambda v: grad_step(h, 0, v))
-        pl.when(h == 1)(d01.relay_b)
+        pl.when(h == 1)(f0.relay)
         each_step(lambda n: product_step(h, 0, n), lambda v: grad_step(h, 1, v))
 
         @pl.when(h == 0)
         def _():
-            d00.send(0, 1)
-            d01.send(0, 1)
-            d00.send(2)
-            d01.send(2)
+            start(*f0.swap, d00.direct[0], d01.direct[0], f0.own[0])
             s1.step(0)
 
         @pl.when(h == 1)
         def _():
-            d10.send(0, 1)
-            d11.send(0, 1)
-            d10.send(2)
-            d11.send(2)
-            d00.end_b()
+            start(*f1.swap, d10.direct[0], d11.direct[0], f1.own[0])
 
         each_step(lambda n: product_step(h, 1, n))
 
     def before_chunk_1():
-        d00.send(3)
-        d01.send(3)
+        start(d00.direct[1], d01.direct[1], f0.own[1])
+        f0.send()
         s1.step(1)
-        d00.relay_b()
         s1.step(2)
 
     staged(H, {1: before_chunk_1}, chunk_step)
-    d10.send(3)
-    d11.send(3)
+    start(d10.direct[1], d11.direct[1], f1.own[1])
+    f1.send()
+    d00.end_b()
     own_stats()
 
     def weight_sent(n, *then):
@@ -483,9 +501,8 @@
 
         return action
 
-    staged(4, {1: weight_sent(0, d01.end_b), 2: weight_sent(1, d10.relay_b), 3: weight_sent(2)}, weight_other)
+    staged(4, {1: weight_sent(0, d01.end_b), 2: weight_sent(1, f1.relay), 3: weight_sent(2)}, weight_other)
     start(weight_copies[3])
-    d11.relay_b()
 
     def before_own_1():
         d00.end_a()
@@ -525,6 +542,7 @@
         pltpu.VMEM((H, 2, 4, HALF, DC), F32),
         pltpu.VMEM((H, 2, 6, HALF, DC), BF16),
         pltpu.VMEM((H, 2, 6, HALF, DC), BF16),
+        pltpu.VMEM((H, 2, HALF, DC), BF16),
         pltpu.VMEM((H, 2, 2, HALF, DC), F32),
         pltpu.VMEM((H, 2, RING - 1, 2, R, DC), BF16),
         pltpu.VMEM((H, 2, RING - 1, 2, R, DC), BF16),
@@ -546,6 +564,7 @@
         pltpu.SemaphoreType.DMA((NSEM,)),
         pltpu.SemaphoreType.DMA((NSEM,)),
         pltpu.SemaphoreType.DMA((H, NZ, 2)),
+        pltpu.SemaphoreType.DMA((H, 2, 2)),
         pltpu.SemaphoreType.DMA((3 + H,)),
     ]
     return pl.pallas_call(

time: 86 us -> 92.4 us (1.074)
  Pallas kernels: 85.3 us -> 91.6 us
    pallas_call x1, Pallas kernels: 83.2 us -> 89.6 us  [call(): pl.pallas_call(kernel, out_shape=(pltpu.VMEM((ROWS, D), F32), pltpu.VMEM(...]
where the time goes in v6:
time: 92.4 us; the launch traced here: 92.3 us
  Pallas kernels  91.6 us (99%)
    pallas_call x1, Pallas kernels, call(): pl.pallas_call(kernel, out_shape=(pltpu.VMEM((ROWS, D), F32), pltpu.VMEM(...  89.6 us
    pallas_call x1, Pallas kernels, store(): pl.pallas_call(store_kernel, out_shape=[jax.ShapeDtypeStruct(a.shape, a.d...  2.06 us

profile of v6, /device:TPU:1, one launch (start us, length us, event | category | flops | bytes accessed | tf_op | source)
XLA Modules:
  0.0 92.3 jit_solution(4242343134977482724)
XLA Ops:
  0.6 89.6 %shard_map.75 = (f32[512,2048]{1,0:T(8,128)S(1)}, f32[2,2,2,16,128]{4,3,2,1,0:T(8,128)S(1)}, f32[1,128]{1,0:T(1,128)S(1)}, f32[1,128]{1,0:T(1,128)S(1)}) custom-call(bf16[2,2,2,16,2048]{4,3,2,1,0:T(8,128)(2,1)} %bitcast.6, bf16[512,2048]{1,0:T(8,128)(2,1)} %w.1, s32[16,128]{1,0:T(8,128)} %bitcast.7, f32[16,128]{1,0:T(8,128)} %bitcast.8), custom_call_target="tpu_custom_call" | custom-call | tf_op jit(solution)/shard_map/pallas_call | solution.py:570
  90.2 2.1 %shard_map.76 = (f32[512,2048]{1,0:T(8,128)}, f32[2,2,2,16,128]{4,3,2,1,0:T(8,128)}, f32[1,128]{1,0:T(1,128)}, f32[1,128]{1,0:T(1,128)}) custom-call(f32[512,2048]{1,0:T(8,128)S(1)} %get-tuple-element.12.refs_0_, f32[2,2,2,16,128]{4,3,2,1,0:T(8,128)S(1)} %get-tuple-element.13.refs_1_, f32[1,128]{1,0:T(1,128)S(1)} %get-tuple-element.14.refs_2_, ...), custom_call_target="tpu_custom_call" | custom-call | tf_op jit(solution)/shard_map/pallas_call | solution.py:596

commit v7 on v5

--- a/solution.py
+++ b/solution.py
@@ -27,7 +27,7 @@
 
 
 def kernel(hid, w, ids, adv, gw_out, gh_out, lp_out, en_out,
-           hall, wall, logits, grad, grad_t, pm, x1, y1, r1, x2, y2, zs, zr, st, sx, sy, sz, fin,
+           hall, wall, logits, grad, grad_t, pm, x1, y1, r1, x2, y2, zs, zr, st, sx, sz, fin,
            ids_in, adv_in, rolled, ids_row, adv_row, stat_swap, gw_send, gw_recv, send_sem, recv_sem, z_sem, local_sem):
     dp, vo = lax.axis_index("dp"), lax.axis_index("vocab")
     x, y = lax.div(dp, RING), lax.rem(dp, RING)
@@ -81,7 +81,8 @@
     bp, _, bm = b_dev
     barrier = pltpu.get_barrier_semaphore()
     z_both = [[dict(dp=dp, vocab=lax.rem(z + k, NZ) * 2 + f) for f in range(2)] for k in range(1, NZ)]
-    peers = a_dev + b_dev + [d for both in z_both for d in both] + [sibling]
+    xy_dev = [dev(lax.rem(pa + i, RING), lax.rem(pb + j, RING)) for i in range(RING) for j in range(RING) if i or j]
+    peers = xy_dev + [d for both in z_both for d in both] + [sibling]
     for peer in peers:
         pl.semaphore_signal(barrier, inc=1, device_id=peer, device_id_type=MESH)
 
@@ -91,21 +92,14 @@
         def __init__(self, h):
             kp, km, k0 = (h * RING + b for b in (b_p, b_m, pb))
             own, there = hid.at[core, h], hall.at[k0, :, pa]
-            self.near = [remote(own, there, d) for d in (ap, am)]
-            self.far = [remote(hall.at[k0, 0, a_m], hall.at[k0, 0, a_m], ap),
-                        remote(hall.at[k0, 1, a_p], hall.at[k0, 1, a_p], am)]
+            self.ring = [remote(own, there, d) for d in (ap, am, a_dev[1])]
             halves = [hall.at[k0, s] for s in range(2)]
             self.first = [remote(halves[0], halves[0], bp), remote(halves[1], halves[1], bm)]
             self.second = [remote(halves[1], halves[1], bp), remote(halves[0], halves[0], bm)]
             self.on = [remote(hall.at[km, 0], hall.at[km, 0], bp), remote(hall.at[kp, 1], hall.at[kp, 1], bm)]
 
-        def ring(self):
-            for near, far in zip(self.near, self.far):
-                arrive(near)
-                start(far)
-
         def spread(self):
-            arrive(*self.far)
+            arrive(*self.ring)
             start(*self.first, *self.second)
 
         def pass_on(self):
@@ -188,8 +182,7 @@
         def __init__(self, h):
             blocks = pl.ds(h * RING, RING)
             self.steps = [(st.at[blocks], sz.at[h], fin.at[0, blocks], z_dev),
-                          (fin.at[0, blocks], sx.at[h], fin.at[1, blocks], a_dev),
-                          (fin.at[1, blocks], sy.at[h], fin.at[2, blocks], b_dev)]
+                          (fin.at[0, blocks], sx.at[h], fin.at[2, blocks], xy_dev)]
             self.sent = [[remote(ref, slots.at[i], d) for i, d in enumerate(devices)]
                          for ref, slots, _, devices in self.steps]
 
@@ -199,12 +192,12 @@
         def step(self, i):
             ref, slots, out, _ = self.steps[i]
             rows = stats_merge(ref, slots, self.sent[i])
-            if i == 2:
+            if i == 1:
                 peak, total, weighted, target = rows
                 rows = (peak + jnp.log(total), weighted / total, target)
             for q, row in enumerate(rows):
                 out[:, pl.ds(q, 1), :] = row
-            if i < 2:
+            if i < 1:
                 start(*self.sent[i + 1])
 
     s0, s1 = Stats(0), Stats(1)
@@ -399,12 +392,10 @@
     reorder(ids_in, ids_row)
     reorder(adv_in, adv_row)
     pl.semaphore_wait(barrier, len(peers))
-    start(*g0.near, *g1.near)
+    start(*g0.ring, *g1.ring)
     for c in [w_in] + own_in:
         c.wait()
     start(w_swap)
-    g0.ring()
-    g1.ring()
     g0.spread()
     g0.pass_on()
     g1.spread()
@@ -430,7 +421,6 @@
 
     staged(4, {1: before_1, 2: before_2, 3: before_3}, unit)
     s1.begin()
-    s0.step(2)
 
     def chunk_step(h):
         each_step(lambda v: grad_step(h, 0, v))
@@ -460,7 +450,6 @@
         d01.send(3)
         s1.step(1)
         d00.relay_b()
-        s1.step(2)
 
     staged(H, {1: before_chunk_1}, chunk_step)
     d10.send(3)
@@ -531,8 +520,7 @@
         pltpu.VMEM((H, NZ, 2, 2, R, 128), F32),
         pltpu.VMEM((H, 2, NZ, 2, R, 128), F32),
         pltpu.VMEM((NB, 4, BLK), F32),
-        pltpu.VMEM((H, RING - 1, RING, 4, BLK), F32),
-        pltpu.VMEM((H, RING - 1, RING, 4, BLK), F32),
+        pltpu.VMEM((H, RING * RING - 1, RING, 4, BLK), F32),
         pltpu.VMEM((H, NZ - 1, RING, 4, BLK), F32),
         pltpu.VMEM((3, NB, 4, BLK), F32),
         pltpu.VMEM((16, 128), jnp.int32),

time: 86 us -> 88.9 us (1.034)
  Pallas kernels: 85.3 us -> 88.2 us
    pallas_call x1, Pallas kernels: 83.2 us -> 86.1 us  [call(): pl.pallas_call(kernel, out_shape=(pltpu.VMEM((ROWS, D), F32), pltpu.VMEM(...]
where the time goes in v7:
time: 88.9 us; the launch traced here: 88.8 us
  Pallas kernels  88.2 us (99%)
    pallas_call x1, Pallas kernels, call(): pl.pallas_call(kernel, out_shape=(pltpu.VMEM((ROWS, D), F32), pltpu.VMEM(...  86.1 us
    pallas_call x1, Pallas kernels, store(): pl.pallas_call(store_kernel, out_shape=[jax.ShapeDtypeStruct(a.shape, a.d...  2.06 us

profile of v7, /device:TPU:1, one launch (start us, length us, event | category | flops | bytes accessed | tf_op | source)
XLA Modules:
  0.0 88.8 jit_solution(1346774060330045780)
XLA Ops:
  0.6 86.1 %shard_map.75 = (f32[512,2048]{1,0:T(8,128)S(1)}, f32[2,2,2,16,128]{4,3,2,1,0:T(8,128)S(1)}, f32[1,128]{1,0:T(1,128)S(1)}, f32[1,128]{1,0:T(1,128)S(1)}) custom-call(bf16[2,2,2,16,2048]{4,3,2,1,0:T(8,128)(2,1)} %bitcast.6, bf16[512,2048]{1,0:T(8,128)(2,1)} %w.1, s32[16,128]{1,0:T(8,128)} %bitcast.7, f32[16,128]{1,0:T(8,128)} %bitcast.8), custom_call_target="tpu_custom_call" | custom-call | tf_op jit(solution)/shard_map/pallas_call | solution.py:539
  86.8 2.1 %shard_map.76 = (f32[512,2048]{1,0:T(8,128)}, f32[2,2,2,16,128]{4,3,2,1,0:T(8,128)}, f32[1,128]{1,0:T(1,128)}, f32[1,128]{1,0:T(1,128)}) custom-call(f32[512,2048]{1,0:T(8,128)S(1)} %get-tuple-element.12.refs_0_, f32[2,2,2,16,128]{4,3,2,1,0:T(8,128)S(1)} %get-tuple-element.13.refs_1_, f32[1,128]{1,0:T(1,128)S(1)} %get-tuple-element.14.refs_2_, ...), custom_call_target="tpu_custom_call" | custom-call | tf_op jit(solution)/shard_map/pallas_call | solution.py:565

commit v8 on v5

--- a/solution.py
+++ b/solution.py
@@ -490,14 +490,15 @@
     def before_own_1():
         d00.end_a()
         z0.send(0)
-        d10.end_b()
 
     def before_own_2():
         d01.end_a()
         z0.send(1)
 
     staged(4, {0: weight_came(0), 1: weight_came(1, before_own_1), 2: weight_came(2, before_own_2),
-               3: weight_came(3, d11.end_b)}, weight_own)
+               3: weight_came(3)}, weight_own)
+    d10.end_b()
+    d11.end_b()
     d10.end_a()
     z1.send(0)
     z0.end()

time: 86 us -> 87.9 us (1.022)
  Pallas kernels: 85.3 us -> 87.1 us
    pallas_call x1, Pallas kernels: 83.2 us -> 85.1 us  [call(): pl.pallas_call(kernel, out_shape=(pltpu.VMEM((ROWS, D), F32), pltpu.VMEM(...]
where the time goes in v8:
time: 87.9 us; the launch traced here: 87.8 us
  Pallas kernels  87.1 us (99%)
    pallas_call x1, Pallas kernels, call(): pl.pallas_call(kernel, out_shape=(pltpu.VMEM((ROWS, D), F32), pltpu.VMEM(...  85.1 us
    pallas_call x1, Pallas kernels, store(): pl.pallas_call(store_kernel, out_shape=[jax.ShapeDtypeStruct(a.shape, a.d...  2.06 us

profile of v8, /device:TPU:1, one launch (start us, length us, event | category | flops | bytes accessed | tf_op | source)
XLA Modules:
  0.0 87.8 jit_solution(7516248885257800860)
XLA Ops:
  0.6 85.1 %shard_map.75 = (f32[512,2048]{1,0:T(8,128)S(1)}, f32[2,2,2,16,128]{4,3,2,1,0:T(8,128)S(1)}, f32[1,128]{1,0:T(1,128)S(1)}, f32[1,128]{1,0:T(1,128)S(1)}) custom-call(bf16[2,2,2,16,2048]{4,3,2,1,0:T(8,128)(2,1)} %bitcast.6, bf16[512,2048]{1,0:T(8,128)(2,1)} %w.1, s32[16,128]{1,0:T(8,128)} %bitcast.7, f32[16,128]{1,0:T(8,128)} %bitcast.8), custom_call_target="tpu_custom_call" | custom-call | tf_op jit(solution)/shard_map/pallas_call | solution.py:552
  85.7 2.1 %shard_map.76 = (f32[512,2048]{1,0:T(8,128)}, f32[2,2,2,16,128]{4,3,2,1,0:T(8,128)}, f32[1,128]{1,0:T(1,128)}, f32[1,128]{1,0:T(1,128)}) custom-call(f32[512,2048]{1,0:T(8,128)S(1)} %get-tuple-element.12.refs_0_, f32[2,2,2,16,128]{4,3,2,1,0:T(8,128)S(1)} %get-tuple-element.13.refs_1_, f32[1,128]{1,0:T(1,128)S(1)} %get-tuple-element.14.refs_2_, ...), custom_call_target="tpu_custom_call" | custom-call | tf_op jit(solution)/shard_map/pallas_call | solution.py:578

commit v9 on v8

--- a/solution.py
+++ b/solution.py
@@ -357,11 +357,11 @@
         return jnp.dot(lhs, rhs, preferred_element_type=F32), cols
 
     def weight_other(n):
-        gw_send[n] = weight_part(1 - core, n)[0]
+        gw_send[n] = weight_part(1 - core, n)[0].astype(BF16)
 
     def weight_own(n):
         part, cols = weight_part(core, n)
-        gw_out[:, cols] = part + gw_recv[n]
+        gw_out[:, cols] = part + gw_recv[n].astype(F32)
 
     stat_copy = remote(stat_swap.at[0], stat_swap.at[1], sibling)
 
@@ -542,8 +542,8 @@
         pltpu.VMEM((NB, 1, BLK), jnp.int32),
         pltpu.VMEM((NB, 1, BLK), F32),
         pltpu.VMEM((2, 2, 8, 128), F32),
-        pltpu.VMEM((D // NC, ROWS, NC), F32),
-        pltpu.VMEM((D // NC, ROWS, NC), F32),
+        pltpu.VMEM((D // NC, ROWS, NC), BF16),
+        pltpu.VMEM((D // NC, ROWS, NC), BF16),
         pltpu.SemaphoreType.DMA((NSEM,)),
         pltpu.SemaphoreType.DMA((NSEM,)),
         pltpu.SemaphoreType.DMA((H, NZ, 2)),

time: 87.9 us -> 85.3 us (0.970)
  Pallas kernels: 87.1 us -> 84 us
    pallas_call x1, Pallas kernels: 85.1 us -> 82 us  [call(): pl.pallas_call(kernel, out_shape=(pltpu.VMEM((ROWS, D), F32), pltpu.VMEM(...]
where the time goes in v9:
time: 85.3 us; the launch traced here: 84.7 us
  Pallas kernels  84 us (98%)
    pallas_call x1, Pallas kernels, call(): pl.pallas_call(kernel, out_shape=(pltpu.VMEM((ROWS, D), F32), pltpu.VMEM(...  82 us
    pallas_call x1, Pallas kernels, store(): pl.pallas_call(store_kernel, out_shape=[jax.ShapeDtypeStruct(a.shape, a.d...  2.06 us

profile of v9, /device:TPU:1, one launch (start us, length us, event | category | flops | bytes accessed | tf_op | source)
XLA Modules:
  0.0 84.7 jit_solution(14486302285598892804)
XLA Ops:
  0.6 82.0 %shard_map.75 = (f32[512,2048]{1,0:T(8,128)S(1)}, f32[2,2,2,16,128]{4,3,2,1,0:T(8,128)S(1)}, f32[1,128]{1,0:T(1,128)S(1)}, f32[1,128]{1,0:T(1,128)S(1)}) custom-call(bf16[2,2,2,16,2048]{4,3,2,1,0:T(8,128)(2,1)} %bitcast.6, bf16[512,2048]{1,0:T(8,128)(2,1)} %w.1, s32[16,128]{1,0:T(8,128)} %bitcast.7, f32[16,128]{1,0:T(8,128)} %bitcast.8), custom_call_target="tpu_custom_call" | custom-call | tf_op jit(solution)/shard_map/pallas_call | solution.py:552
  82.6 2.1 %shard_map.76 = (f32[512,2048]{1,0:T(8,128)}, f32[2,2,2,16,128]{4,3,2,1,0:T(8,128)}, f32[1,128]{1,0:T(1,128)}, f32[1,128]{1,0:T(1,128)}) custom-call(f32[512,2048]{1,0:T(8,128)S(1)} %get-tuple-element.12.refs_0_, f32[2,2,2,16,128]{4,3,2,1,0:T(8,128)S(1)} %get-tuple-element.13.refs_1_, f32[1,128]{1,0:T(1,128)S(1)} %get-tuple-element.14.refs_2_, ...), custom_call_target="tpu_custom_call" | custom-call | tf_op jit(solution)/shard_map/pallas_call | solution.py:578
